TPU v7x, 256 devices: a whole 4x4x8 slice. The times are simulated.
256 devices in a mesh: grp: 8 (over x, core), dev: 32 (over z, y).
Axes of the slice: x: 4, y: 4, z: 8, core: 2. Of those that a mesh axis runs over, the one named last changes fastest.
Arguments:
- home_points: bfloat16 [524288, 512], P(('grp', 'dev')), may hold values from -6 to 6
- counts: int32 [256], P(('grp', 'dev')), may hold values from 0 to 2, as said below
- owner_group: int32 [512], P(('grp', 'dev')), may hold values from 0 to 7, as said below
- neighbors_home: int32 [27, 524288], P(None, ('grp', 'dev')), may hold values from 0 to 1023
- hilbert_target: int32 [4096], P(('grp', 'dev')), may hold values from 0 to 511, as said below
- neighbors_second: int32 [27, 262144], P(None, ('grp', 'dev')), may hold values from 0 to 1023
- depth_first: float32 [27, 512], replicated, may hold values from -1.5 to 1.5
- mixing_first: bfloat16 [512, 512], replicated, may hold values from -0.25 to 0.25
- gain_first: float32 [512], replicated, may hold values from 0.1 to 1.9
- w_qkv_first: bfloat16 [512, 1536], replicated, may hold values from -3 to 3
- w_out_first: bfloat16 [512, 512], replicated, may hold values from -0.25 to 0.25
- depth_second: float32 [27, 512], replicated, may hold values from -1.5 to 1.5
- mixing_second: bfloat16 [512, 512], replicated, may hold values from -0.25 to 0.25
- gain_second: float32 [512], replicated, may hold values from 0.1 to 1.9
- w_qkv_second: bfloat16 [512, 1536], replicated, may hold values from -3 to 3
- w_out_second: bfloat16 [512, 512], replicated, may hold values from -0.25 to 0.25
Outputs:
- encoded_points: bfloat16 [524288, 512], P(('grp', 'dev'))
Inputs may be any that keep to these rules, and one draw needn't show every extreme that they name: For each dev index, the counts of its 8 tiles sum to 8. `owner_group`: the live slots of one tile name distinct groups, and for each dev index d and group q exactly one live slot of the tiles with dev index d names q. Dead slots' values are unused. `hilbert_target`: within each group the targets are a permutation of 0 to 511, and at most 2 blocks of one device name the same device (target // 16).
All inputs are finite; a program needn't handle non-finite values.
Results may differ from a plain program's by a relative error of at most 0.025.
Values may be sent and summed in bfloat16 or wider, within the bound.
No kernel may reach another device: no remote copies, remote signals or barrier semaphores. Data moves between devices by JAX's collectives and lax.ppermute only.
A program may use at most 128 MiB of HBM per device.

v0:
```python
import jax
import jax.numpy as jnp
from jax import lax
from jax.sharding import PartitionSpec as P

HEADS = 8
HEAD_DIM = 64
CAPACITY = 2


epsilon = 1e-05


def encoder_block(features, neighbours, params):
    depth, mixing, gain, w_qkv, w_out = params
    patch_rows, width = features.shape
    gathered = jnp.zeros(features.shape, jnp.float32)
    for which in range(neighbours.shape[0]):
        gathered = gathered + features[neighbours[which]].astype(jnp.float32) * depth[which]
    encoded = gathered.astype(jnp.bfloat16)
    updated = features.astype(jnp.float32) + jnp.dot(
        encoded, mixing, preferred_element_type=jnp.float32
    )
    centre = jnp.mean(updated, axis=-1, keepdims=True)
    spread = jnp.mean((updated - centre) ** 2, axis=-1, keepdims=True)
    normed = ((updated - centre) * lax.rsqrt(spread + epsilon) * gain).astype(jnp.bfloat16)
    project = jnp.dot(normed, w_qkv, preferred_element_type=jnp.float32).astype(jnp.bfloat16)
    portions = 8
    portion_width = width // portions
    portion_heads = HEADS // portions

    def attend(portion):
        start = portion * portion_width
        queries = lax.dynamic_slice_in_dim(project, start, portion_width, 1).reshape(
            patch_rows, portion_heads, HEAD_DIM
        )
        keyside = lax.dynamic_slice_in_dim(project, width + start, portion_width, 1).reshape(
            patch_rows, portion_heads, HEAD_DIM
        )
        values = lax.dynamic_slice_in_dim(project, 2 * width + start, portion_width, 1).reshape(
            patch_rows, portion_heads, HEAD_DIM
        )
        scores = jnp.einsum(
            "qhd,khd->hqk", queries, keyside, preferred_element_type=jnp.float32
        ) * HEAD_DIM ** (-0.5)
        peaks = jnp.max(scores, axis=-1, keepdims=True)
        powers = jnp.exp(scores - peaks)
        totals = jnp.sum(powers, axis=-1, keepdims=True)
        weights = (powers / totals).astype(jnp.bfloat16)
        mixed = jnp.einsum("hqk,khd->qhd", weights, values, preferred_element_type=jnp.float32)
        return mixed.reshape(patch_rows, portion_width).astype(jnp.bfloat16)

    pieces = lax.map(attend, jnp.arange(portions))
    mixed = jnp.transpose(pieces, (1, 0, 2)).reshape(patch_rows, width)
    return (updated + jnp.dot(mixed, w_out, preferred_element_type=jnp.float32)).astype(
        jnp.bfloat16
    )


def run_blocks(features, lists, params):
    return lax.map(lambda pair: encoder_block(pair[0], pair[1], params), (features, lists))


def outbound(data, picked, present):
    shaped = present.reshape((present.shape[0],) + (1,) * (data.ndim - 1))
    return jnp.where(shaped, data[picked], jnp.zeros((), data.dtype))


def body(
    home_points,
    counts,
    owner_group,
    neighbors_home,
    hilbert_target,
    neighbors_second,
    depth_first,
    mixing_first,
    gain_first,
    w_qkv_first,
    w_out_first,
    depth_second,
    mixing_second,
    gain_second,
    w_qkv_second,
    w_out_second,
):
    groups = lax.axis_size("grp")
    owners = lax.axis_size("dev")
    home_rows, width = home_points.shape
    slot_count = owner_group.shape[0]
    patch_rows = home_rows // slot_count
    block_count = hilbert_target.shape[0]
    block_rows = patch_rows // block_count
    fanout = neighbors_home.shape[0]
    first_params = (depth_first, mixing_first, gain_first, w_qkv_first, w_out_first)
    second_params = (depth_second, mixing_second, gain_second, w_qkv_second, w_out_second)
    tiles = home_points.reshape(slot_count, patch_rows, width)
    tile_lists = jnp.transpose(neighbors_home.reshape(fanout, slot_count, patch_rows), (1, 0, 2))
    filled = jnp.arange(slot_count) < counts[0]
    match = filled[None, :] & (owner_group[None, :] == jnp.arange(groups)[:, None])
    present = jnp.any(match, axis=1)
    picked = jnp.sum(jnp.where(match, jnp.arange(slot_count)[None, :], 0), axis=1)
    marker = present.astype(jnp.int32)
    computed = run_blocks(tiles, tile_lists, first_params)
    arrived, senders = (
        lax.all_to_all(
            outbound(computed, picked, present), "grp", split_axis=0, concat_axis=0, tiled=True
        ),
        lax.all_to_all(marker, "grp", split_axis=0, concat_axis=0, tiled=True),
    )
    anchor = jnp.sum(jnp.arange(groups) * senders)
    section_one = lax.dynamic_index_in_dim(arrived, anchor, 0, keepdims=False)
    pieces = section_one.reshape(block_count, block_rows, width)
    destination = hilbert_target // block_count
    position = hilbert_target % block_count
    counter = jnp.arange(block_count)
    same_dest = destination[:, None] == destination[None, :]
    rank = jnp.sum(same_dest & (counter[:, None] > counter[None, :]), axis=1)
    place = destination * CAPACITY + rank
    buffer_slots = owners * CAPACITY
    table = place[None, :] == jnp.arange(buffer_slots)[:, None]
    occupied = jnp.any(table, axis=1)
    source_block = jnp.sum(jnp.where(table, counter[None, :], 0), axis=1)
    outgoing = jnp.where(occupied[:, None, None], pieces[source_block], jnp.zeros((), jnp.bfloat16))
    outgoing = outgoing.reshape(owners, CAPACITY, block_rows, width)
    labels = jnp.where(occupied, position[source_block], -1).reshape(owners, CAPACITY)
    incoming, incoming_labels = (
        lax.all_to_all(outgoing, "dev", split_axis=0, concat_axis=0, tiled=True),
        lax.all_to_all(labels, "dev", split_axis=0, concat_axis=0, tiled=True),
    )
    incoming_flat = incoming.reshape(buffer_slots, block_rows, width)
    label_flat = incoming_labels.reshape(buffer_slots)
    hits = label_flat[None, :] == counter[:, None]
    fetch = jnp.sum(jnp.where(hits, jnp.arange(buffer_slots)[None, :], 0), axis=1)
    regrouped = incoming_flat[fetch].reshape(1, patch_rows, width)
    second_lists = neighbors_second.reshape(1, fanout, patch_rows)
    section_two = run_blocks(regrouped, second_lists, second_params)[0].reshape(
        block_count, block_rows, width
    )
    backward = jnp.where(
        (label_flat >= 0)[:, None, None],
        section_two[jnp.maximum(label_flat, 0)],
        jnp.zeros((), jnp.bfloat16),
    )
    backward = backward.reshape(owners, CAPACITY, block_rows, width)
    returned = lax.all_to_all(backward, "dev", split_axis=0, concat_axis=0, tiled=True).reshape(
        buffer_slots, block_rows, width
    )
    finished = returned[place].reshape(patch_rows, width)
    homeward = jnp.where(
        (jnp.arange(groups) == anchor)[:, None, None], finished[None], jnp.zeros((), jnp.bfloat16)
    )
    delivered = lax.all_to_all(homeward, "grp", split_axis=0, concat_axis=0, tiled=True)
    result = jnp.where(filled[:, None, None], delivered[owner_group], jnp.zeros((), jnp.bfloat16))
    return result.reshape(home_rows, width)


def solution(mesh):
    return jax.shard_map(
        body,
        mesh=mesh,
        in_specs=(
            P(("grp", "dev"), None),
            P(("grp", "dev")),
            P(("grp", "dev")),
            P(None, ("grp", "dev")),
            P(("grp", "dev")),
            P(None, ("grp", "dev")),
            P(),
            P(),
            P(),
            P(),
            P(),
            P(),
            P(),
            P(),
            P(),
            P(),
        ),
        out_specs=P(("grp", "dev"), None),
        check_vma=False,
    )
```

profile of v0, /device:TPU:1, one launch (start us, length us, event | category | flops | bytes accessed | tf_op | source)
XLA Modules:
  0.0 1198.5 jit_solution(4656845194627109251)
XLA Ops:
  2.7 7.1 all-to-all-start
  12.3 493.9 %while.51 = (s32[]{:T(128)}, bf16[2,1024,512]{2,1,0:T(8,128)(2,1)}, bf16[2,1024,512]{2,1,0:T(8,128)(2,1)}, s32[2,27,1024]{2,0,1:T(2,128)S(1)}, f32[27,512]{1,0:T...) while((s32[]{:T(128)}, bf16[2,1024,512]{2,1,0:T(8,128)(2,1)}, ...), condition=%wide.region_12.13_spmd, body=%wide.region_5.0_spmd.sunk | while | flops 3012733952 | bytes 154494320 | solution.py:61
  13.7 5.1 gather_fusion
  18.9 5.1 gather_fusion.1
  23.9 5.1 gather_fusion.2
  39.1 5.1 gather_fusion.5
  84.7 5.1 gather_fusion.14
  110.0 5.1 gather_fusion.19
  120.1 5.1 gather_fusion.21
  125.2 5.1 gather_fusion.22
  130.3 5.1 gather_fusion.23
  145.5 5.1 gather_fusion.26
  153.2 14.5 %fusion.101 = (f32[1024]{0:T(1024)S(1)}, f32[1024,512]{0,1:T(8,128)}) fusion(bf16[512,512]{1,0:T(8,128)(2,1)} %get-tuple-element.832, bf16[1024,512]{1,0:T(8,128)(2,1)} %gather_fusion, bf16[1024,512]{1,0:T(8,128)(2,1)} %gather_fusion.1, bf16[1024,512]{1,0:T(8,128)(2,1)} %gather_fusion.2, bf16[1024,512]{1,0:T(8,128)(2,1)} %gather_fusion.3, ...), kind=kOutput, calls=%fused_computation.324.clone.1 | convolution fusion | flops 580910080 | bytes 32040960 | tf_op jit(solution)/shard_map/while/body/eval_jaxpr/dot_general | solution.py:21
  175.0 73.1 %while.53 = (s32[]{:T(128)}, bf16[8,1024,64]{1,2,0:T(8,128)(2,1)S(1)}, s32[8]{0:T(128)S(1)}, bf16[1024,1536]{1,0:T(8,128)(2,1)}, s32[]{:T(128)}, /*index=5*/s32[...) while((s32[]{:T(128)}, ...), condition=%wide.region_11.11_spmd, body=%wide.region_8.10_spmd.sunk | while | flops 277936128 | bytes 30298428 | solution.py:53
  255.4 5.1 gather_fusion
  260.6 5.1 gather_fusion.1
  265.7 5.1 gather_fusion.2
  280.9 5.1 gather_fusion.5
  326.4 5.1 gather_fusion.14
  351.7 5.1 gather_fusion.19
  361.9 5.1 gather_fusion.21
  366.9 5.1 gather_fusion.22
  372.0 5.1 gather_fusion.23
  387.2 5.1 gather_fusion.26
  395.0 14.5 %fusion.101 = (f32[1024]{0:T(1024)S(1)}, f32[1024,512]{0,1:T(8,128)}) fusion(bf16[512,512]{1,0:T(8,128)(2,1)} %get-tuple-element.832, bf16[1024,512]{1,0:T(8,128)(2,1)} %gather_fusion, bf16[1024,512]{1,0:T(8,128)(2,1)} %gather_fusion.1, bf16[1024,512]{1,0:T(8,128)(2,1)} %gather_fusion.2, bf16[1024,512]{1,0:T(8,128)(2,1)} %gather_fusion.3, ...), kind=kOutput, calls=%fused_computation.324.clone.1 | convolution fusion | flops 580910080 | bytes 32040960 | tf_op jit(solution)/shard_map/while/body/eval_jaxpr/dot_general | solution.py:21
  416.8 73.1 %while.53 = (s32[]{:T(128)}, bf16[8,1024,64]{1,2,0:T(8,128)(2,1)S(1)}, s32[8]{0:T(128)S(1)}, bf16[1024,1536]{1,0:T(8,128)(2,1)}, s32[]{:T(128)}, /*index=5*/s32[...) while((s32[]{:T(128)}, ...), condition=%wide.region_11.11_spmd, body=%wide.region_8.10_spmd.sunk | while | flops 277936128 | bytes 30298428 | solution.py:53
  506.2 6.0 gather_fusion.28
  512.3 7.2 broadcast_select_fusion
  519.5 5.1 all-to-all-start.2
  530.3 88.1 %all-to-all-done.2 = bf16[8,1024,512]{2,1,0:T(8,128)(2,1)} async-done(((bf16[8,1024,512]{2,1,0:T(8,128)(2,1)}), bf16[8,1024,512]{2,1,0:T(8,128)(2,1)}, u32[]{:S(2)}, u32[]{:S(2)}) %all-to-all-start.2) | async-done | bytes 8388640 | tf_op jit(solution)/shard_map/all_to_all | solution.py:106
  618.4 9.9 all-to-all-start.1
  636.8 9.5 all-to-all-start.3
  648.8 89.7 %all-to-all-done.3 = bf16[32,2,64,512]{3,2,1,0:T(8,128)(2,1)} async-done(((bf16[32,2,64,512]{3,2,1,0:T(8,128)(2,1)}), bf16[32,2,64,512]{3,2,1,0:T(8,128)(2,1)}, u32[]{:S(2)}, u32[]{:S(2)}) %all-to-all-start.3) | async-done | bytes 4194336 | tf_op jit(solution)/shard_map/all_to_all | solution.py:128
  741.3 5.1 gather_fusion.57
  746.4 5.1 gather_fusion.56
  756.5 5.1 gather_fusion.54
  781.8 5.1 gather_fusion.49
  822.3 5.1 gather_fusion.41
  847.5 5.1 gather_fusion.36
  857.6 5.1 gather_fusion.34
  867.8 5.1 gather_fusion.32
  877.9 14.5 %fusion.69 = (f32[1024]{0:T(1024)S(1)}, f32[1024,512]{1,0:T(8,128)S(1)}) fusion(bf16[512,512]{1,0:T(8,128)(2,1)} %param.34, bf16[1024,512]{1,0:T(8,128)(2,1)} %gather_fusion.57, bf16[1024,512]{1,0:T(8,128)(2,1)} %gather_fusion.56, bf16[1024,512]{1,0:T(8,128)(2,1)} %gather_fusion.55, bf16[1024,512]{1,0:T(8,128)(2,1)} %gather_fusion.54, ...), kind=kOutput, calls=%fused_computation.327 | convolution fusion | flops 580910080 | bytes 32040960 | tf_op jit(solution)/shard_map/while/body/eval_jaxpr/dot_general | solution.py:21
  896.7 73.3 %while.52 = (s32[]{:T(128)}, bf16[8,1024,64]{1,2,0:T(8,128)(2,1)S(1)}, s32[8]{0:T(128)S(1)}, bf16[1024,1536]{1,0:T(8,128)(2,1)}, s32[]{:T(128)}, /*index=5*/s32[...) while((s32[]{:T(128)}, ...), condition=%wide.region_20.21_spmd, body=%wide.region_17.20_spmd.sunk | while | flops 277936128 | bytes 30298428 | solution.py:53
  980.9 8.2 all-to-all-start.4
  989.8 91.4 %all-to-all-done.4 = bf16[32,2,64,512]{3,2,1,0:T(8,128)(2,1)} async-done(((bf16[32,2,64,512]{3,2,1,0:T(8,128)(2,1)}), bf16[32,2,64,512]{3,2,1,0:T(8,128)(2,1)}, u32[]{:S(2)}, u32[]{:S(2)}) %all-to-all-start.4) | async-done | bytes 4194336 | tf_op jit(solution)/shard_map/all_to_all | solution.py:146
  1087.8 8.2 all-to-all-start.5
  1096.2 93.7 %all-to-all-done.5 = bf16[8,1024,512]{2,1,0:T(8,128)(2,1)} async-done(((bf16[8,1024,512]{2,1,0:T(8,128)(2,1)}), bf16[8,1024,512]{2,1,0:T(8,128)(2,1)}, u32[]{:S(2)}, u32[]{:S(2)}) %all-to-all-start.5) | async-done | bytes 8388640 | tf_op jit(solution)/shard_map/all_to_all | solution.py:153
  1189.9 5.5 gather_fusion.60
  (417 shorter events, 552.8 us)
Async XLA Ops:
  0.0 892.9 %copy-start = (bf16[512,1536]{1,0:T(8,128)(2,1)S(1)}, bf16[512,1536]{1,0:T(8,128)(2,1)}, u32[]{:S(2)}) copy-start(bf16[512,1536]{1,0:T(8,128)(2,1)} %param.36) | copy-start | bytes 4718596
  0.8 11.5 copy-start.14
  2.7 516.8 %all-to-all-start = ((s32[8,1,1]{2,1,0:T(1,128)}), s32[8,1,1]{2,1,0:T(1,128)}, u32[]{:S(2)}, u32[]{:S(2)}) async-start(s32[8,1,1]{2,1,0:T(1,128)} %copy.211), calls=%async_computation | async-start | bytes 8192 | tf_op jit(solution)/shard_map/all_to_all | solution.py:109
  12.2 494.0 %copy-start.20 = (s32[8]{0:T(128)S(1)}, s32[8]{0:T(128)}, u32[]{:S(2)}) copy-start(s32[8]{0:T(128)} %select_reduce_fusion.2) | copy-start | bytes 100
  145.5 5.1 copy-start.6
  167.7 2.0 copy-start.16
  167.7 2.2 copy-start.3
  175.0 73.1 %copy-start.4 = (bf16[512,512]{1,0:T(8,128)(2,1)S(1)}, bf16[512,512]{1,0:T(8,128)(2,1)}, u32[]{:S(2)}) copy-start(bf16[512,512]{1,0:T(8,128)(2,1)} %get-tuple-element.835) | copy-start | bytes 1572868 | tf_op jit(solution)/shard_map/while
  178.1 1.9 copy-start.1
  187.3 1.9 copy-start.1
  196.4 1.9 copy-start.1
  205.6 1.9 copy-start.1
  214.7 1.9 copy-start.1
  223.8 1.9 copy-start.1
  233.0 1.9 copy-start.1
  242.1 1.9 copy-start.1
  387.2 5.1 copy-start.6
  409.5 2.0 copy-start.16
  409.5 2.2 copy-start.3
  416.8 73.1 %copy-start.4 = (bf16[512,512]{1,0:T(8,128)(2,1)S(1)}, bf16[512,512]{1,0:T(8,128)(2,1)}, u32[]{:S(2)}) copy-start(bf16[512,512]{1,0:T(8,128)(2,1)} %get-tuple-element.835) | copy-start | bytes 1572868 | tf_op jit(solution)/shard_map/while
  419.9 1.9 copy-start.1
  429.0 1.9 copy-start.1
  438.2 1.9 copy-start.1
  447.3 1.9 copy-start.1
  456.4 1.9 copy-start.1
  465.6 1.9 copy-start.1
  474.7 1.9 copy-start.1
  483.9 1.9 copy-start.1
  506.2 6.1 copy-start.13
  519.5 5.1 copy-start.18
  519.5 98.9 %all-to-all-start.2 = ((bf16[8,1024,512]{2,1,0:T(8,128)(2,1)}), bf16[8,1024,512]{2,1,0:T(8,128)(2,1)}, u32[]{:S(2)}, u32[]{:S(2)}) async-start(bf16[8,1024,512]{2,1,0:T(8,128)(2,1)} %broadcast_select_fusion), calls=%async_computation.2 | async-start | bytes 16777216 | tf_op jit(solution)/shard_map/all_to_all | solution.py:106
  618.4 18.4 %all-to-all-start.1 = ((s32[32,1,2]{2,1,0:T(1,128)}), s32[32,1,2]{2,1,0:T(1,128)S(1)}, u32[]{:S(2)}, u32[]{:S(2)}) async-start(s32[32,1,2]{2,1,0:T(1,128)} %bitcast.97), calls=%async_computation.1 | async-start | bytes 32768 | tf_op jit(solution)/shard_map/all_to_all | solution.py:129
  636.8 9.5 copy-start.10
  636.8 10.0 copy-start.11
  636.8 101.7 %all-to-all-start.3 = ((bf16[32,2,64,512]{3,2,1,0:T(8,128)(2,1)}), bf16[32,2,64,512]{3,2,1,0:T(8,128)(2,1)}, u32[]{:S(2)}, u32[]{:S(2)}) async-start(bf16[32,2,64,512]{3,2,1,0:T(8,128)(2,1)} %broadcast_select_fusion.2), calls=%async_computation.3 | async-start | bytes 8388608 | tf_op jit(solution)/shard_map/all_to_all | solution.py:128
  892.4 4.3 copy-start.5
  893.1 3.6 copy-start.7
  896.7 74.3 %copy-start.9 = (bf16[512,512]{1,0:T(8,128)(2,1)S(1)}, bf16[512,512]{1,0:T(8,128)(2,1)}, u32[]{:S(2)}) copy-start(bf16[512,512]{1,0:T(8,128)(2,1)} %param.37) | copy-start | bytes 1572868
  899.8 1.9 copy-start.2
  909.0 1.9 copy-start.2
  918.2 1.9 copy-start.2
  927.3 1.9 copy-start.2
  936.5 1.9 copy-start.2
  964.0 1.9 copy-start.2
  980.9 100.3 %all-to-all-start.4 = ((bf16[32,2,64,512]{3,2,1,0:T(8,128)(2,1)}), bf16[32,2,64,512]{3,2,1,0:T(8,128)(2,1)}, u32[]{:S(2)}, u32[]{:S(2)}) async-start(bf16[32,2,64,512]{3,2,1,0:T(8,128)(2,1)} %broadcast_select_fusion.3), calls=%async_computation.4 | async-start | bytes 8388608 | tf_op jit(solution)/shard_map/all_to_all | solution.py:146
  1087.8 8.2 copy-start.15
  1087.8 8.3 copy-start.19
  1087.8 102.1 %all-to-all-start.5 = ((bf16[8,1024,512]{2,1,0:T(8,128)(2,1)}), bf16[8,1024,512]{2,1,0:T(8,128)(2,1)}, u32[]{:S(2)}, u32[]{:S(2)}) async-start(bf16[8,1024,512]{2,1,0:T(8,128)(2,1)} %broadcast_select_fusion.1), calls=%async_computation.5 | async-start | bytes 16777216 | tf_op jit(solution)/shard_map/all_to_all | solution.py:153
  (5 other events, 6.1 us)
where the time goes:
time: 1220 us; the launch traced here: 1200 us
  local copies, waits for them, and re-layouts  515 us (42%)
  waiting for transfers between devices  363 us (30%)
  matrix products  191 us (16%)
  other arithmetic  51.2 us (4%)
  starting transfers between devices  47.9 us (4%)
  loops' own time  27 us (2%)
    gather x81, local copies, waits for them, and re-layouts, encoder_block(): features[neighbours[which]].astype(jnp.float32) * depth[which]  410 us
    all_to_all x1, waiting for transfers between devices, body(): lax.all_to_all(homeward, 'grp', split_axis=0, concat_axis=0, tiled=True)  93.7 us
    all_to_all x1, waiting for transfers between devices, body(): lax.all_to_all(backward, 'dev', split_axis=0, concat_axis=0, tiled=True)  91.4 us
    all_to_all x1, waiting for transfers between devices, body(): lax.all_to_all(outgoing, 'dev', split_axis=0, concat_axis=0, tiled=True)  89.7 us
    all_to_all x1, waiting for transfers between devices, body(): lax.all_to_all(outbound(computed, picked, present), 'grp', split_axis=0,...  88.1 us
    dot_general x24, matrix products, attend(): jnp.einsum('hqk,khd->qhd', weights, values, preferred_element_type=jnp.fl...  80.2 us
    while x64, local copies, waits for them, and re-layouts  46.5 us
    dot_general x24, matrix products, attend(): jnp.einsum('qhd,khd->hqk', queries, keyside, preferred_element_type=jnp.f...  44.1 us
  transfers between devices with their start and end apart: 6, of which 4 were waited for; matrix products, arithmetic and copies ran while one was open for 39% of the time, Pallas kernels for 0%

commit v1 on v0

v1 whole, which is shorter than its diff:
```python
import functools
import jax, jax.numpy as jnp
from jax import lax
from jax.experimental import pallas as pl
from jax.experimental.pallas import tpu as pltpu
from jax.sharding import PartitionSpec as P

HEADS = 8
HEAD_DIM = 64
epsilon = 1e-05
SCALE = HEAD_DIM ** (-0.5) * 1.4426950408889634
UNROLL = 8
TILE = 256


def block_kernel(arrives_split, lists, x_ref, depth_ref, mixing_ref, gain_ref, w_qkv_ref, w_out_ref, out_ref, plain, summed, updated, project, mixed):
    rows, width = x_ref.shape
    fanout = depth_ref.shape[0]
    lanes = 128
    chunks = width // lanes
    side = 32
    for c in range(chunks):
        cols = slice(c * lanes, (c + 1) * lanes)
        if arrives_split:
            for i in range(side):
                plain[pl.ds(i * chunks + c, side, stride=side * chunks), :] = x_ref[i * side : (i + 1) * side, cols].astype(jnp.float32)
        else:
            plain[pl.ds(c, rows, stride=chunks), :] = x_ref[:, cols].astype(jnp.float32)

    def gather(step, carry):
        first = step * UNROLL
        for u in range(UNROLL):
            total = None
            for j in range(fanout):
                start = lists[(first + u) * fanout + j]
                term = plain[pl.ds(start, chunks), :] * depth_ref[j]
                total = term if total is None else total + term
            summed[pl.ds(pl.multiple_of((first + u) * chunks, chunks), chunks), :] = total
        return carry

    lax.fori_loop(0, rows // UNROLL, gather, 0)

    def head(tile, carry):
        row0 = pl.multiple_of(tile * TILE, TILE)
        encoded = jnp.concatenate(
            [summed[pl.ds(row0 * chunks + c, TILE, stride=chunks), :] for c in range(chunks)], axis=1
        ).astype(jnp.bfloat16)
        groups = TILE // side
        residual = jnp.concatenate(
            [
                jnp.concatenate(
                    [plain[pl.ds((tile * groups + g) * chunks + c, side, stride=side * chunks), :] for g in range(groups)], axis=0
                )
                for c in range(chunks)
            ],
            axis=1,
        )
        up = residual + jnp.dot(encoded, mixing_ref[...], preferred_element_type=jnp.float32)
        updated[pl.ds(row0, TILE), :] = up
        centre = jnp.mean(up, axis=-1, keepdims=True)
        off = up - centre
        spread = jnp.mean(off * off, axis=-1, keepdims=True)
        normed = (off * lax.rsqrt(spread + epsilon) * gain_ref[...]).astype(jnp.bfloat16)
        project[pl.ds(row0, TILE), :width] = (
            jnp.dot(normed, w_qkv_ref[:, :width], preferred_element_type=jnp.float32) * SCALE
        ).astype(jnp.bfloat16)
        project[pl.ds(row0, TILE), width:] = jnp.dot(
            normed, w_qkv_ref[:, width:], preferred_element_type=jnp.float32
        ).astype(jnp.bfloat16)
        return carry

    lax.fori_loop(0, rows // TILE, head, 0)
    left = lax.broadcasted_iota(jnp.int32, (TILE, lanes), 1) < HEAD_DIM
    ones = jnp.ones((rows, lanes), jnp.bfloat16)
    for pair in range(width // lanes):
        cols = slice(pair * lanes, (pair + 1) * lanes)
        keys = project[:, width + pair * lanes : width + (pair + 1) * lanes]
        values = jnp.concatenate([project[:, 2 * width + pair * lanes : 2 * width + (pair + 1) * lanes], ones], axis=1)

        def attend(tile, carry):
            row0 = pl.multiple_of(tile * TILE, TILE)
            queries = project[pl.ds(row0, TILE), cols]
            results = []
            for half in range(2):
                keep = left if half == 0 else jnp.logical_not(left)
                own = jnp.where(keep, queries, jnp.zeros((), jnp.bfloat16))
                scores = lax.dot_general(own, keys, (((1,), (1,)), ((), ())), preferred_element_type=jnp.float32)
                peak = jnp.max(scores, axis=-1, keepdims=True)
                powers = jnp.exp2(scores - peak).astype(jnp.bfloat16)
                both = jnp.dot(powers, values, preferred_element_type=jnp.float32)
                results.append(both[:, :lanes] / both[:, lanes:])
            mixed[pl.ds(row0, TILE), cols] = jnp.where(left, results[0], results[1]).astype(jnp.bfloat16)
            return carry

        lax.fori_loop(0, rows // TILE, attend, 0)

    def tail(tile, carry):
        row0 = pl.multiple_of(tile * TILE, TILE)
        out_ref[pl.ds(row0, TILE), :] = (
            updated[pl.ds(row0, TILE), :]
            + jnp.dot(mixed[pl.ds(row0, TILE), :], w_out_ref[...], preferred_element_type=jnp.float32)
        ).astype(jnp.bfloat16)
        return carry

    lax.fori_loop(0, rows // TILE, tail, 0)


def encoder_block(features, lists, params, arrives_split):
    depth, mixing, gain, w_qkv, w_out = params
    rows, width = features.shape
    fanout = depth.shape[0]
    vmem = pl.BlockSpec(memory_space=pltpu.VMEM)
    return pl.pallas_call(
        functools.partial(block_kernel, arrives_split),
        out_shape=jax.ShapeDtypeStruct((rows, width), jnp.bfloat16),
        in_specs=[pl.BlockSpec(memory_space=pltpu.SMEM)] + [vmem] * 6,
        out_specs=vmem,
        scratch_shapes=[
            pltpu.VMEM((rows * 4, 128), jnp.float32),
            pltpu.VMEM((rows * 4, 128), jnp.float32),
            pltpu.VMEM((rows, width), jnp.float32),
            pltpu.VMEM((rows, 3 * width), jnp.bfloat16),
            pltpu.VMEM((rows, width), jnp.bfloat16),
        ],
        compiler_params=pltpu.CompilerParams(vmem_limit_bytes=48 << 20),
        cost_estimate=pl.CostEstimate(flops=5_000_000_000, bytes_accessed=6_000_000, transcendentals=8_000_000),
        name="block",
    )(lists, features, depth.reshape(fanout, 4, 128), mixing, gain.reshape(1, width), w_qkv, w_out)


def permute_kernel(x_ref, source_ref, out_ref):
    rows = x_ref.shape[0]
    positions = lax.broadcasted_iota(jnp.int32, (TILE, rows), 1)
    for tile in range(rows // TILE):
        own = slice(tile * TILE, (tile + 1) * TILE)
        chosen = jnp.where(positions == source_ref[own, :], 1.0, 0.0).astype(jnp.bfloat16)
        out_ref[own, :] = jnp.dot(chosen, x_ref[...], preferred_element_type=jnp.float32).astype(jnp.bfloat16)


def permute_rows(x, source):
    vmem = pl.BlockSpec(memory_space=pltpu.VMEM)
    return pl.pallas_call(
        permute_kernel,
        out_shape=jax.ShapeDtypeStruct(x.shape, x.dtype),
        in_specs=[vmem, vmem],
        out_specs=vmem,
        compiler_params=pltpu.CompilerParams(vmem_limit_bytes=32 << 20),
        cost_estimate=pl.CostEstimate(flops=1_100_000_000, bytes_accessed=2_100_000, transcendentals=0),
        name="permute",
    )(x, source.reshape(-1, 1))


def exchange(x, axis):
    return lax.all_to_all(x, axis, split_axis=0, concat_axis=0, tiled=True)


def body(
    home_points,
    counts,
    owner_group,
    neighbors_home,
    hilbert_target,
    neighbors_second,
    depth_first,
    mixing_first,
    gain_first,
    w_qkv_first,
    w_out_first,
    depth_second,
    mixing_second,
    gain_second,
    w_qkv_second,
    w_out_second,
):
    groups = lax.axis_size("grp")
    owners = lax.axis_size("dev")
    home_rows, width = home_points.shape
    slots = owner_group.shape[0]
    rows = home_rows // slots
    blocks = hilbert_target.shape[0]
    fanout = neighbors_home.shape[0]
    part = rows // groups
    side = rows // owners
    first_params = (depth_first, mixing_first, gain_first, w_qkv_first, w_out_first)
    second_params = (depth_second, mixing_second, gain_second, w_qkv_second, w_out_second)

    plan = lax.all_gather(jnp.concatenate([counts, owner_group]), "grp", axis=0, tiled=False)
    live = jnp.arange(slots)[None, :] < plan[:, :1]
    owner = plan[:, 1:].reshape(-1)
    live = live.reshape(-1)
    match = live[None, :] & (owner[None, :] == jnp.arange(groups)[:, None])
    source = jnp.sum(jnp.where(match, jnp.arange(groups * slots)[None, :], 0), axis=1)
    target = lax.all_gather(hilbert_target, "dev", axis=0, tiled=True)
    pieces = target.shape[0]
    inverse = jnp.sum(
        jnp.where(target[None, :] == jnp.arange(pieces)[:, None], jnp.arange(pieces)[None, :], 0), axis=1
    )
    pair = jnp.arange(2)[None, :]
    forward_rows = (2 * inverse[:, None] + pair).reshape(-1)
    backward_rows = (2 * target[:, None] + pair).reshape(-1)

    def ordered(lists):
        return jnp.transpose(lists.reshape(fanout, -1, owners, owners), (1, 3, 2, 0))

    home_lists = ordered(neighbors_home).reshape(slots, 2, -1)
    packed = home_lists[:, 0] + home_lists[:, 1] * 65536
    packed = jnp.transpose(packed.reshape(slots, groups, -1), (1, 0, 2))
    second_lists = ordered(neighbors_second).reshape(-1) * 4

    points = jnp.transpose(home_points.reshape(slots, groups, part, width), (1, 0, 2, 3))
    spread = exchange(points, "grp").reshape(groups * slots, part, width)
    spread_lists = exchange(packed, "grp").reshape(groups * slots, -1)
    owned = exchange(spread[source], "grp").reshape(rows, width)
    owned_lists = exchange(spread_lists[source], "grp").reshape(-1)
    first_lists = jnp.concatenate([owned_lists & 65535, owned_lists >> 16]) * 4

    section_one = encoder_block(owned, first_lists, first_params, False)
    mid = exchange(section_one.reshape(owners, side, width), "dev").reshape(rows, width)
    mid = permute_rows(mid, forward_rows)
    regrouped = exchange(mid.reshape(owners, side, width), "dev").reshape(rows, width)
    section_two = encoder_block(regrouped, second_lists, second_params, True)
    mid = exchange(section_two.reshape(owners, side, width), "dev").reshape(rows, width)
    mid = permute_rows(mid, backward_rows)
    returned = exchange(mid.reshape(owners, side, width), "dev").reshape(groups, part, width)
    gathered = exchange(returned, "grp")
    homeward = jnp.where(live[:, None, None], gathered[owner], jnp.zeros((), jnp.bfloat16))
    delivered = exchange(homeward.reshape(groups, slots, part, width), "grp")
    result = delivered.reshape(groups, slots, owners // groups, side, width)
    return jnp.transpose(result, (1, 3, 0, 2, 4)).reshape(home_rows, width)


def solution(mesh):
    return jax.shard_map(
        body,
        mesh=mesh,
        in_specs=(
            P(("grp", "dev"), None),
            P(("grp", "dev")),
            P(("grp", "dev")),
            P(None, ("grp", "dev")),
            P(("grp", "dev")),
            P(None, ("grp", "dev")),
            P(),
            P(),
            P(),
            P(),
            P(),
            P(),
            P(),
            P(),
            P(),
            P(),
        ),
        out_specs=P(("grp", "dev"), None),
        check_vma=False,
    )
```

time: 1220 us -> 383 us (0.31); the launches traced: 1200 us -> 382 us
  local copies, waits for them, and re-layouts: 515 us -> 23.8 us
  waiting for transfers between devices: 363 us -> 77.7 us
  matrix products: 191 us -> 0 us
  blocking collectives: 0 us -> 115 us
  Pallas kernels: 0 us -> 108 us
  other arithmetic: 51.2 us -> 1.79 us
  loops' own time: 27 us -> 0 us
    gather x88 -> x3, local copies, waits for them, and re-layouts: 433 us -> 4.59 us  [the longest x1 3.33 us: body(): owned = exchange(spread[source], 'grp').reshape(rows, width)]
    all_to_all x6 -> x8, waiting for transfers between devices: 363 us -> 77.7 us  [exchange(): return lax.all_to_all(x, axis, split_axis=0, concat_axis=0, tiled=True)]
    dot_general x57 -> x0, matrix products: 191 us -> none  [the longest x24 80.2 us: attend(): jnp.einsum('hqk,khd->qhd', weights, values, preferred_element_type=jnp.fl...]
    pallas_call x0 -> x4, Pallas kernels: none -> 108 us  [the longest x2 104 us: encoder_block(): pl.pallas_call(functools.partial(block_kernel, arrives_split), out_shape=...]
    all_to_all x0 -> x2, blocking collectives: none -> 59.7 us  [exchange(): return lax.all_to_all(x, axis, split_axis=0, concat_axis=0, tiled=True)]
    unnamed x0 -> x2, blocking collectives: none -> 55.1 us
    while x64 -> x0, local copies, waits for them, and re-layouts: 46.5 us -> none
    another operation x4 -> x0, loops' own time: 27 us -> none  [the longest x3 16.3 us: encoder_block(): pieces = lax.map(attend, jnp.arange(portions))]
  transfers between devices with their start and end apart: 6 -> 8, of which waited for: 4 -> 6; matrix products, arithmetic and copies ran while one was open for 39% -> 4% of each run, Pallas kernels for 0% -> 0%
where the time goes in v1:
time: 383 us; the launch traced here: 382 us
  blocking collectives  115 us (30%)
  Pallas kernels  108 us (28%)
  waiting for transfers between devices  77.7 us (20%)
  starting transfers between devices  53.6 us (14%)
  local copies, waits for them, and re-layouts  23.8 us (6%)
    pallas_call x2, Pallas kernels, encoder_block(): pl.pallas_call(functools.partial(block_kernel, arrives_split), out_shape=...  104 us
    all_to_all x8, waiting for transfers between devices, exchange(): return lax.all_to_all(x, axis, split_axis=0, concat_axis=0, tiled=True)  77.7 us
    all_to_all x2, blocking collectives, exchange(): return lax.all_to_all(x, axis, split_axis=0, concat_axis=0, tiled=True)  59.7 us
    unnamed x2, blocking collectives  55.1 us
    all_to_all x8, starting transfers between devices, exchange(): return lax.all_to_all(x, axis, split_axis=0, concat_axis=0, tiled=True)  53.6 us
  transfers between devices with their start and end apart: 8, of which 6 were waited for; matrix products, arithmetic and copies ran while one was open for 4% of the time, Pallas kernels for 0%

profile of v1, /device:TPU:1, one launch (start us, length us, event | category | flops | bytes accessed | tf_op | source)
XLA Modules:
  0.0 381.7 jit_solution(9401610482200670184)
XLA Ops:
  0.0 1.2 reshape.205
  1.2 1.1 copy.38
  2.4 0.8 reshape.206
  3.2 0.4 fusion.1
  3.7 0.7 copy.39
  4.4 6.5 %all-to-all-start = ((s32[8,2,1728]{2,1,0:T(2,128)}), s32[8,2,1728]{2,1,0:T(2,128)S(1)}, u32[]{:S(2)}, u32[]{:S(2)}) async-start(s32[8,2,1728]{2,1,0:T(2,128)} %copy.39), calls=%async_computation | async-start | bytes 229376 | tf_op jit(solution)/shard_map/all_to_all | solution.py:154
  10.9 1.5 copy.41
  12.4 3.6 all-to-all-done
  16.0 4.3 %all-to-all-start.2 = ((bf16[8,2,128,512]{3,2,1,0:T(8,128)(2,1)}), bf16[8,2,128,512]{3,2,1,0:T(8,128)(2,1)S(1)}, u32[]{:S(2)}, u32[]{:S(2)}) async-start(bf16[8,2,128,512]{3,2,1,0:T(8,128)(2,1)} %copy.41), calls=%async_computation.2 | async-start | bytes 4194304 | tf_op jit(solution)/shard_map/all_to_all | solution.py:154
  21.1 0.6 dynamic-slice
  22.3 0.2 add_dynamic-update-slice_fusion
  22.5 26.0 %all-reduce = s32[24]{0:T(128)S(1)} all-reduce(s32[24]{0:T(128)S(1)} %add_dynamic-update-slice_fusion), channel_id=2, replica_groups=mesh['grp'=8,'dev'=32] {'grp'}, use_global_device_ids=true, to_apply=%add | all-reduce | flops 24 | bytes 192
  49.2 0.6 gather_fusion
  49.8 0.7 copy.40
  50.5 5.3 %all-to-all-start.1 = ((s32[8,1,1728]{2,1,0:T(1,128)}), s32[8,1,1728]{2,1,0:T(1,128)S(1)}, u32[]{:S(2)}, u32[]{:S(2)}) async-start(s32[8,1,1728]{2,1,0:T(1,128)} %copy.40), calls=%async_computation.1 | async-start | bytes 114688 | tf_op jit(solution)/shard_map/all_to_all | solution.py:154
  55.8 3.3 gather_fusion.1
  59.1 1.5 all-to-all-done.1
  60.6 4.2 %all-to-all-start.3 = ((bf16[8,128,512]{2,1,0:T(8,128)(2,1)}), bf16[8,128,512]{2,1,0:T(8,128)(2,1)S(1)}, u32[]{:S(2)}, u32[]{:S(2)}) async-start(bf16[8,128,512]{2,1,0:T(8,128)(2,1)} %gather_fusion.1), calls=%async_computation.3 | async-start | bytes 2097152 | tf_op jit(solution)/shard_map/all_to_all | solution.py:154
  64.9 0.3 and_reduce_fusion
  65.4 14.6 %all-to-all-done.3 = bf16[8,128,512]{2,1,0:T(8,128)(2,1)S(1)} async-done(((bf16[8,128,512]{2,1,0:T(8,128)(2,1)}), bf16[8,128,512]{2,1,0:T(8,128)(2,1)S(1)}, u32[]{:S(2)}, u32[]{:S(2)}) %all-to-all-start.3) | async-done | bytes 1048608 | tf_op jit(solution)/shard_map/all_to_all | solution.py:154
  80.0 1.0 copy-done.3
  81.0 51.2 %block.2 = bf16[1024,512]{1,0:T(8,128)(2,1)} custom-call(s32[27648]{0:T(1024)S(1)} %add_multiply_fusion.lists, bf16[1024,512]{1,0:T(8,128)(2,1)S(1)} %bitcast.36, f32[27,4,128]{2,1,0:T(4,128)S(1)} %reshape.211.depth_ref, bf16[512,512]{1,0:T(8,128)(2,1)S(1)} %copy-done.2, f32[1,512]{1,0:T(1,128)S(1)} %bitcast.40, bf16[512,1536]{1,0:T(8,128)(2,1)S(1)} %copy-done, ...), custom_call_target="tpu_custom_call" | custom-call | flops 5000000000 | bytes 6000000 | tf_op jit(solution)/shard_map/block/pallas_call | solution.py:113
  132.2 10.6 %all-to-all-start.4 = ((bf16[32,32,512]{2,1,0:T(8,128)(2,1)}), bf16[32,32,512]{2,1,0:T(8,128)(2,1)S(1)}, u32[]{:S(2)}, u32[]{:S(2)}) async-start(bf16[32,32,512]{2,1,0:T(8,128)(2,1)} %bitcast.12), calls=%async_computation.4 | async-start | bytes 2097152 | tf_op jit(solution)/shard_map/all_to_all | solution.py:154
  142.9 0.6 dynamic-slice.1
  144.1 0.2 dynamic-update-slice.1
  144.4 29.1 %all-reduce.1 = s32[512]{0:T(512)S(1)} all-reduce(s32[512]{0:T(512)S(1)} %dynamic-update-slice.1), channel_id=1, replica_groups=mesh['grp'=8,'dev'=32] {'dev'}, use_global_device_ids=true, to_apply=%add.1 | all-reduce | flops 512 | bytes 4096
  173.5 0.2 select_reduce_fusion
  173.8 0.1 add.90.source_ref
  174.0 2.3 permute.2
  176.3 6.9 %all-to-all-start.5 = ((bf16[32,32,512]{2,1,0:T(8,128)(2,1)}), bf16[32,32,512]{2,1,0:T(8,128)(2,1)S(1)}, u32[]{:S(2)}, u32[]{:S(2)}) async-start(bf16[32,32,512]{2,1,0:T(8,128)(2,1)} %bitcast.15), calls=%async_computation.5 | async-start | bytes 2097152 | tf_op jit(solution)/shard_map/all_to_all | solution.py:154
  183.2 0.9 mul.33
  184.1 2.3 copy.37
  186.5 1.4 mul.35.lists
  187.9 19.6 %all-to-all-done.5 = bf16[32,32,512]{2,1,0:T(8,128)(2,1)S(1)} async-done(((bf16[32,32,512]{2,1,0:T(8,128)(2,1)}), bf16[32,32,512]{2,1,0:T(8,128)(2,1)S(1)}, u32[]{:S(2)}, u32[]{:S(2)}) %all-to-all-start.5) | async-done | bytes 1048608 | tf_op jit(solution)/shard_map/all_to_all | solution.py:154
  207.5 1.0 copy-done.5
  208.5 52.9 %block.3 = bf16[1024,512]{1,0:T(8,128)(2,1)} custom-call(s32[27648]{0:T(1024)S(1)} %mul.35.lists, bf16[1024,512]{1,0:T(8,128)(2,1)S(1)} %bitcast.37, f32[27,4,128]{2,1,0:T(4,128)S(1)} %reshape.217.depth_ref, bf16[512,512]{1,0:T(8,128)(2,1)S(1)} %copy-done.4, f32[1,512]{1,0:T(1,128)S(1)} %bitcast.41, bf16[512,1536]{1,0:T(8,128)(2,1)S(1)} %copy-done.1, ...), custom_call_target="tpu_custom_call" | custom-call | flops 5000000000 | bytes 6000000 | tf_op jit(solution)/shard_map/block/pallas_call | solution.py:113
  261.5 6.6 %all-to-all-start.6 = ((bf16[32,32,512]{2,1,0:T(8,128)(2,1)}), bf16[32,32,512]{2,1,0:T(8,128)(2,1)S(1)}, u32[]{:S(2)}, u32[]{:S(2)}) async-start(bf16[32,32,512]{2,1,0:T(8,128)(2,1)} %bitcast.18), calls=%async_computation.6 | async-start | bytes 2097152 | tf_op jit(solution)/shard_map/all_to_all | solution.py:154
  268.2 0.1 add.91.source_ref
  268.3 23.5 %all-to-all-done.6 = bf16[32,32,512]{2,1,0:T(8,128)(2,1)S(1)} async-done(((bf16[32,32,512]{2,1,0:T(8,128)(2,1)}), bf16[32,32,512]{2,1,0:T(8,128)(2,1)S(1)}, u32[]{:S(2)}, u32[]{:S(2)}) %all-to-all-start.6) | async-done | bytes 1048608 | tf_op jit(solution)/shard_map/all_to_all | solution.py:154
  291.8 1.3 permute.3
  293.1 29.9 %all_to_all.54 = bf16[32,32,512]{2,1,0:T(8,128)(2,1)} all-to-all(bf16[32,32,512]{2,1,0:T(8,128)(2,1)S(1)} %bitcast.39), channel_id=1, replica_groups=mesh['grp'=8,'dev'=32] {'dev'}, dimensions={0} | all-to-all | bytes 2097152 | tf_op jit(solution)/shard_map/all_to_all | solution.py:154
  323.0 9.2 %all-to-all-start.8 = ((bf16[8,128,512]{2,1,0:T(8,128)(2,1)}), bf16[8,128,512]{2,1,0:T(8,128)(2,1)S(1)}, u32[]{:S(2)}, u32[]{:S(2)}) async-start(bf16[8,128,512]{2,1,0:T(8,128)(2,1)} %bitcast.21), calls=%async_computation.8 | async-start | bytes 2097152 | tf_op jit(solution)/shard_map/all_to_all | solution.py:154
  332.3 15.0 %all-to-all-done.8 = bf16[8,128,512]{2,1,0:T(8,128)(2,1)S(1)} async-done(((bf16[8,128,512]{2,1,0:T(8,128)(2,1)}), bf16[8,128,512]{2,1,0:T(8,128)(2,1)S(1)}, u32[]{:S(2)}, u32[]{:S(2)}) %all-to-all-start.8) | async-done | bytes 1048608 | tf_op jit(solution)/shard_map/all_to_all | solution.py:154
  347.3 0.7 gather_fusion.2
  348.0 0.2 broadcast_select_fusion
  348.2 29.8 %all_to_all.55 = bf16[8,2,128,512]{3,2,1,0:T(8,128)(2,1)S(1)} all-to-all(bf16[8,2,128,512]{3,2,1,0:T(8,128)(2,1)S(1)} %broadcast_select_fusion), channel_id=1, replica_groups=mesh['grp'=8,'dev'=32] {'grp'}, dimensions={0} | all-to-all | bytes 4194304 | tf_op jit(solution)/shard_map/all_to_all | solution.py:154
  378.0 1.6 copy.44
  379.6 2.0 reshape.225
  (60 shorter events, 1.5 us)
Async XLA Ops:
  2.4 8.5 %copy-start.9 = (bf16[2048,512]{1,0:T(8,128)(2,1)S(1)}, bf16[2048,512]{1,0:T(8,128)(2,1)}, u32[]{:S(2)}) copy-start(bf16[2048,512]{1,0:T(8,128)(2,1)} %param.16) | copy-start | bytes 6291460
  4.4 11.6 %all-to-all-start = ((s32[8,2,1728]{2,1,0:T(2,128)}), s32[8,2,1728]{2,1,0:T(2,128)S(1)}, u32[]{:S(2)}, u32[]{:S(2)}) async-start(s32[8,2,1728]{2,1,0:T(2,128)} %copy.39), calls=%async_computation | async-start | bytes 229376 | tf_op jit(solution)/shard_map/all_to_all | solution.py:154
  12.4 8.6 %copy-start.16 = (u32[256]{0:T(256)S(1)}, u32[256]{0:T(256)}, u32[]{:S(2)}) copy-start(u32[256]{0:T(256)} %constant.24) | copy-start | bytes 3076
  12.4 9.9 %copy-start.13 = (s32[2]{0:T(128)S(1)}, s32[2]{0:T(128)}, u32[]{:S(2)}) copy-start(s32[2]{0:T(128)} %param.18) | copy-start | bytes 28
  16.0 34.4 %all-to-all-start.2 = ((bf16[8,2,128,512]{3,2,1,0:T(8,128)(2,1)}), bf16[8,2,128,512]{3,2,1,0:T(8,128)(2,1)S(1)}, u32[]{:S(2)}, u32[]{:S(2)}) async-start(bf16[8,2,128,512]{3,2,1,0:T(8,128)(2,1)} %copy.41), calls=%async_computation.2 | async-start | bytes 4194304 | tf_op jit(solution)/shard_map/all_to_all | solution.py:154
  50.5 5.3 %copy-start.8 = (bf16[8,2,128,512]{3,2,1,0:T(8,128)(2,1)}, bf16[8,2,128,512]{3,2,1,0:T(8,128)(2,1)S(1)}, u32[]{:S(2)}) copy-start(bf16[8,2,128,512]{3,2,1,0:T(8,128)(2,1)S(1)} %all-to-all-done.2) | copy-start | bytes 6291460
  50.5 10.1 %all-to-all-start.1 = ((s32[8,1,1728]{2,1,0:T(1,128)}), s32[8,1,1728]{2,1,0:T(1,128)S(1)}, u32[]{:S(2)}, u32[]{:S(2)}) async-start(s32[8,1,1728]{2,1,0:T(1,128)} %copy.40), calls=%async_computation.1 | async-start | bytes 114688 | tf_op jit(solution)/shard_map/all_to_all | solution.py:154
  55.8 9.1 %copy-start.11 = (f32[27,512]{1,0:T(8,128)S(1)}, f32[27,512]{1,0:T(8,128)}, u32[]{:S(2)}) copy-start(f32[27,512]{1,0:T(8,128)} %param.22) | copy-start | bytes 165892
  55.8 24.2 %copy-start = (bf16[512,1536]{1,0:T(8,128)(2,1)S(1)}, bf16[512,1536]{1,0:T(8,128)(2,1)}, u32[]{:S(2)}) copy-start(bf16[512,1536]{1,0:T(8,128)(2,1)} %w_qkv_ref.2) | copy-start | bytes 4718596
  55.8 24.2 %copy-start.2 = (bf16[512,512]{1,0:T(8,128)(2,1)S(1)}, bf16[512,512]{1,0:T(8,128)(2,1)}, u32[]{:S(2)}) copy-start(bf16[512,512]{1,0:T(8,128)(2,1)} %mixing_ref.2) | copy-start | bytes 1572868
  55.8 24.2 %copy-start.6 = (f32[512]{0:T(512)S(1)}, f32[512]{0:T(512)}, u32[]{:S(2)}) copy-start(f32[512]{0:T(512)} %param.24) | copy-start | bytes 6148
  60.6 19.3 %all-to-all-start.3 = ((bf16[8,128,512]{2,1,0:T(8,128)(2,1)}), bf16[8,128,512]{2,1,0:T(8,128)(2,1)S(1)}, u32[]{:S(2)}, u32[]{:S(2)}) async-start(bf16[8,128,512]{2,1,0:T(8,128)(2,1)} %gather_fusion.1), calls=%async_computation.3 | async-start | bytes 2097152 | tf_op jit(solution)/shard_map/all_to_all | solution.py:154
  80.0 1.0 copy-start.3
  132.2 10.6 %copy-start.15 = (u32[256]{0:T(256)S(1)}, u32[256]{0:T(256)}, u32[]{:S(2)}) copy-start(u32[256]{0:T(256)} %constant.29) | copy-start | bytes 3076
  132.2 11.9 %copy-start.14 = (s32[16]{0:T(128)S(1)}, s32[16]{0:T(128)}, u32[]{:S(2)}) copy-start(s32[16]{0:T(128)} %param.20) | copy-start | bytes 196
  132.2 41.8 %all-to-all-start.4 = ((bf16[32,32,512]{2,1,0:T(8,128)(2,1)}), bf16[32,32,512]{2,1,0:T(8,128)(2,1)S(1)}, u32[]{:S(2)}, u32[]{:S(2)}) async-start(bf16[32,32,512]{2,1,0:T(8,128)(2,1)} %bitcast.12), calls=%async_computation.4 | async-start | bytes 2097152 | tf_op jit(solution)/shard_map/all_to_all | solution.py:154
  174.0 9.2 %copy-start.10 = (s32[27,1024]{1,0:T(8,128)S(1)}, s32[27,1024]{1,0:T(8,128)}, u32[]{:S(2)}) copy-start(s32[27,1024]{1,0:T(8,128)} %param.21) | copy-start | bytes 331780
  176.3 11.6 %copy-start.12 = (f32[27,512]{1,0:T(8,128)S(1)}, f32[27,512]{1,0:T(8,128)}, u32[]{:S(2)}) copy-start(f32[27,512]{1,0:T(8,128)} %param.27) | copy-start | bytes 165892
  176.3 31.2 %copy-start.1 = (bf16[512,1536]{1,0:T(8,128)(2,1)S(1)}, bf16[512,1536]{1,0:T(8,128)(2,1)}, u32[]{:S(2)}) copy-start(bf16[512,1536]{1,0:T(8,128)(2,1)} %w_qkv_ref.3) | copy-start | bytes 4718596
  176.3 31.2 %copy-start.4 = (bf16[512,512]{1,0:T(8,128)(2,1)S(1)}, bf16[512,512]{1,0:T(8,128)(2,1)}, u32[]{:S(2)}) copy-start(bf16[512,512]{1,0:T(8,128)(2,1)} %mixing_ref.3) | copy-start | bytes 1572868
  176.3 31.2 %copy-start.7 = (f32[512]{0:T(512)S(1)}, f32[512]{0:T(512)}, u32[]{:S(2)}) copy-start(f32[512]{0:T(512)} %param.29) | copy-start | bytes 6148
  176.3 31.2 %all-to-all-start.5 = ((bf16[32,32,512]{2,1,0:T(8,128)(2,1)}), bf16[32,32,512]{2,1,0:T(8,128)(2,1)S(1)}, u32[]{:S(2)}, u32[]{:S(2)}) async-start(bf16[32,32,512]{2,1,0:T(8,128)(2,1)} %bitcast.15), calls=%async_computation.5 | async-start | bytes 2097152 | tf_op jit(solution)/shard_map/all_to_all | solution.py:154
  207.5 1.0 copy-start.5
  261.5 30.4 %all-to-all-start.6 = ((bf16[32,32,512]{2,1,0:T(8,128)(2,1)}), bf16[32,32,512]{2,1,0:T(8,128)(2,1)S(1)}, u32[]{:S(2)}, u32[]{:S(2)}) async-start(bf16[32,32,512]{2,1,0:T(8,128)(2,1)} %bitcast.18), calls=%async_computation.6 | async-start | bytes 2097152 | tf_op jit(solution)/shard_map/all_to_all | solution.py:154
  323.0 24.3 %all-to-all-start.8 = ((bf16[8,128,512]{2,1,0:T(8,128)(2,1)}), bf16[8,128,512]{2,1,0:T(8,128)(2,1)S(1)}, u32[]{:S(2)}, u32[]{:S(2)}) async-start(bf16[8,128,512]{2,1,0:T(8,128)(2,1)} %bitcast.21), calls=%async_computation.8 | async-start | bytes 2097152 | tf_op jit(solution)/shard_map/all_to_all | solution.py:154

commit v2 on v1

v2 whole, which is shorter than its diff:
```python
import functools
import jax
import jax.numpy as jnp
from jax import lax
from jax.experimental import pallas as pl
from jax.experimental.pallas import tpu as pltpu
from jax.sharding import PartitionSpec as P

HEADS = 8
HEAD_DIM = 64
epsilon = 1e-05
SCALE = HEAD_DIM ** (-0.5) * 1.4426950408889634
LANES = 128
TILE = 256
SIDE = 32
CHUNK = 128
BUFFERS = 2
LIST_ROWS = 14


def block_kernel(first, *refs):
    if first:
        (
            x_ref, depth_ref, mixing_ref, gain_ref, w_qkv_ref, w_out_ref, out_ref,
            plain, summed, updated, project, mixed, scores_even, scores_odd, lists_ref, *stage
        ) = refs
    else:
        (
            lists_ref, x_ref, depth_ref, mixing_ref, gain_ref, w_qkv_ref, w_out_ref, out_ref,
            plain, summed, updated, project, mixed, scores_even, scores_odd, *stage
        ) = refs
    buffers, sems = stage[:BUFFERS], stage[BUFFERS]
    rows, width = out_ref.shape
    fanout = depth_ref.shape[0]
    chunks = width // LANES
    pairs = width // LANES
    tiles = rows // TILE
    count = rows // CHUNK
    if first:
        parts = x_ref.shape[0]
        part = rows // parts
        halves = parts // 4

        def digits(block):
            upper = x_ref[2 * block, part : part + LIST_ROWS, :]
            lower = x_ref[2 * block + 1, part : part + LIST_ROWS, :]
            return upper.astype(jnp.float32), lower.astype(jnp.float32)

        for half in range(halves):
            high, low = digits(half), digits(halves + half)
            for piece in range(2):
                found = ((high[piece] * 32.0 + low[piece]) * chunks).astype(jnp.int32)
                kept = min(LIST_ROWS, fanout - piece * LIST_ROWS)
                for c in range(chunks):
                    lists_ref[half * chunks + c, piece * LIST_ROWS : piece * LIST_ROWS + kept, :] = found[
                        :kept, c * LANES : (c + 1) * LANES
                    ]

    def fetch(chunk, slot):
        return pltpu.make_async_copy(lists_ref.at[chunk], buffers[slot], sems.at[slot])

    for slot in range(BUFFERS):
        fetch(slot, slot).start()
    for c in range(chunks):
        cols = slice(c * LANES, (c + 1) * LANES)
        if first:
            for p in range(parts):
                plain[pl.ds(p * part * chunks + c, part, stride=chunks), :] = x_ref[p, :part, cols].astype(jnp.float32)
        else:
            plain[pl.ds(c, rows, stride=chunks), :] = x_ref[:, cols].astype(jnp.float32)

    def gather(step, carry):
        for slot in range(BUFFERS):
            chunk = step * BUFFERS + slot
            fetch(chunk, slot).wait()
            base = pl.multiple_of(chunk * (CHUNK // SIDE) * chunks, (CHUNK // SIDE) * chunks)
            for u in range(CHUNK):
                total = None
                for j in range(fanout):
                    term = plain[pl.ds(buffers[slot][j, u], chunks), :] * depth_ref[j]
                    total = term if total is None else total + term
                summed[pl.ds(base + ((u % SIDE) * SIDE + u // SIDE) * chunks, chunks), :] = total

            @pl.when(chunk + BUFFERS < count)
            def _():
                fetch(chunk + BUFFERS, slot).start()

        return carry

    lax.fori_loop(0, count // BUFFERS, gather, 0)

    def head(tile, carry):
        row0 = pl.multiple_of(tile * TILE, TILE)
        encoded = jnp.concatenate(
            [summed[pl.ds(row0 * chunks + c, TILE, stride=chunks), :] for c in range(chunks)], axis=1
        ).astype(jnp.bfloat16)
        if first:
            groups = TILE // SIDE
            residual = jnp.concatenate(
                [
                    jnp.concatenate(
                        [
                            plain[pl.ds((tile * groups + g) * chunks + c, SIDE, stride=SIDE * chunks), :]
                            for g in range(groups)
                        ],
                        axis=0,
                    )
                    for c in range(chunks)
                ],
                axis=1,
            )
        else:
            residual = x_ref[pl.ds(row0, TILE), :].astype(jnp.float32)
        up = residual + jnp.dot(encoded, mixing_ref[...], preferred_element_type=jnp.float32)
        updated[pl.ds(row0, TILE), :] = up
        centre = jnp.mean(up, axis=-1, keepdims=True)
        off = up - centre
        spread = jnp.mean(off * off, axis=-1, keepdims=True)
        normed = (off * lax.rsqrt(spread + epsilon) * gain_ref[...]).astype(jnp.bfloat16)
        project[pl.ds(row0, TILE), :width] = (
            jnp.dot(normed, w_qkv_ref[:, :width], preferred_element_type=jnp.float32) * SCALE
        ).astype(jnp.bfloat16)
        project[pl.ds(row0, TILE), width:] = jnp.dot(
            normed, w_qkv_ref[:, width:], preferred_element_type=jnp.float32
        ).astype(jnp.bfloat16)
        return carry

    lax.fori_loop(0, tiles, head, 0)
    left = lax.broadcasted_iota(jnp.int32, (TILE, LANES), 1) < HEAD_DIM
    ones = jnp.ones((rows, LANES), jnp.bfloat16)

    def place(step):
        row0 = pl.multiple_of(lax.rem(step, tiles) * TILE, TILE)
        col0 = pl.multiple_of(lax.div(step, tiles) * LANES, LANES)
        return row0, col0

    def score(step, half, target):
        row0, col0 = place(step)
        queries = project[pl.ds(row0, TILE), pl.ds(col0, LANES)]
        keep = left if half == 0 else jnp.logical_not(left)
        own = jnp.where(keep, queries, jnp.zeros((), jnp.bfloat16))
        keys = project[:, pl.ds(width + col0, LANES)]
        target[...] = lax.dot_general(own, keys, (((1,), (1,)), ((), ())), preferred_element_type=jnp.float32)

    def weigh(step, source):
        row0, col0 = place(step)
        scores = source[...]
        values = jnp.concatenate([project[:, pl.ds(2 * width + col0, LANES)], ones], axis=1)
        peak = jnp.max(scores, axis=-1, keepdims=True)
        powers = jnp.exp2(scores - peak).astype(jnp.bfloat16)
        both = jnp.dot(powers, values, preferred_element_type=jnp.float32)
        return both[:, :LANES] / both[:, LANES:]

    score(0, 0, scores_even)

    def attend(step, carry):
        row0, col0 = place(step)
        score(step, 1, scores_odd)
        left_result = weigh(step, scores_even)
        score(jnp.minimum(step + 1, pairs * tiles - 1), 0, scores_even)
        right_result = weigh(step, scores_odd)
        mixed[pl.ds(row0, TILE), pl.ds(col0, LANES)] = jnp.where(left, left_result, right_result).astype(jnp.bfloat16)
        return carry

    lax.fori_loop(0, pairs * tiles, attend, 0)

    def tail(tile, carry):
        row0 = pl.multiple_of(tile * TILE, TILE)
        out_ref[pl.ds(row0, TILE), :] = (
            updated[pl.ds(row0, TILE), :]
            + jnp.dot(mixed[pl.ds(row0, TILE), :], w_out_ref[...], preferred_element_type=jnp.float32)
        ).astype(jnp.bfloat16)
        return carry

    lax.fori_loop(0, tiles, tail, 0)


def encoder_block(features, lists, params, rows):
    depth, mixing, gain, w_qkv, w_out = params
    fanout, width = depth.shape
    first = lists is None
    vmem = pl.BlockSpec(memory_space=pltpu.VMEM)
    table = (rows // CHUNK, SIDE, LANES)
    operands = (features, depth.reshape(fanout, -1, LANES), mixing, gain.reshape(1, width), w_qkv, w_out)
    if not first:
        operands = (lists,) + operands
    return pl.pallas_call(
        functools.partial(block_kernel, first),
        out_shape=jax.ShapeDtypeStruct((rows, width), jnp.bfloat16),
        in_specs=[vmem] * len(operands),
        out_specs=vmem,
        scratch_shapes=[
            pltpu.VMEM((rows * 4, LANES), jnp.float32),
            pltpu.VMEM((rows * 4, LANES), jnp.float32),
            pltpu.VMEM((rows, width), jnp.float32),
            pltpu.VMEM((rows, 3 * width), jnp.bfloat16),
            pltpu.VMEM((rows, width), jnp.bfloat16),
            pltpu.VMEM((TILE, rows), jnp.float32),
            pltpu.VMEM((TILE, rows), jnp.float32),
        ]
        + [pltpu.VMEM(table, jnp.int32)] * first
        + [pltpu.SMEM(table[1:], jnp.int32)] * BUFFERS
        + [pltpu.SemaphoreType.DMA((BUFFERS,))],
        compiler_params=pltpu.CompilerParams(vmem_limit_bytes=48 << 20),
        cost_estimate=pl.CostEstimate(flops=5_000_000_000, bytes_accessed=6_000_000, transcendentals=8_000_000),
        name="block",
    )(*operands)


def staged(lists, rows):
    fanout = lists.shape[0]
    table = jnp.transpose((lists * 4).reshape(fanout, rows // CHUNK, LANES), (1, 0, 2))
    return jnp.pad(table, ((0, 0), (0, SIDE - fanout), (0, 0)))


def enclosed(neighbors, plan, slots, groups, width):
    fanout = neighbors.shape[0]
    lists = jnp.transpose(neighbors.reshape(fanout, slots, -1, width), (1, 2, 0, 3))
    lists = jnp.pad(lists, ((0, 0), (0, 0), (0, 2 * LIST_ROWS - fanout), (0, 0)))
    letters = jnp.concatenate([lists // 32, lists % 32], axis=1).reshape(slots, groups, LIST_ROWS, width)
    note = jnp.broadcast_to(jnp.pad(plan, (0, width - plan.shape[0])), (slots, groups, 2, width))
    return jnp.concatenate([letters, note], axis=2).astype(jnp.bfloat16)


def permute_kernel(x_ref, source_ref, out_ref):
    rows = x_ref.shape[0]
    positions = lax.broadcasted_iota(jnp.int32, (TILE, rows), 1)
    for tile in range(rows // TILE):
        own = slice(tile * TILE, (tile + 1) * TILE)
        chosen = jnp.where(positions == source_ref[own, :], 1.0, 0.0).astype(jnp.bfloat16)
        out_ref[own, :] = jnp.dot(chosen, x_ref[...], preferred_element_type=jnp.float32).astype(jnp.bfloat16)


def permute_rows(x, source):
    vmem = pl.BlockSpec(memory_space=pltpu.VMEM)
    return pl.pallas_call(
        permute_kernel,
        out_shape=jax.ShapeDtypeStruct(x.shape, x.dtype),
        in_specs=[vmem, vmem],
        out_specs=vmem,
        compiler_params=pltpu.CompilerParams(vmem_limit_bytes=32 << 20),
        cost_estimate=pl.CostEstimate(flops=1_100_000_000, bytes_accessed=2_100_000, transcendentals=0),
        name="permute",
    )(x, source.reshape(-1, 1))


def pick_kernel(source_ref, x_ref, out_ref, sems):
    copies = [
        pltpu.make_async_copy(x_ref.at[source_ref[q]], out_ref.at[q], sems.at[q]) for q in range(out_ref.shape[0])
    ]
    for copy in copies:
        copy.start()
    for copy in copies:
        copy.wait()


def pick_parts(x, source):
    count = source.shape[0]
    return pl.pallas_call(
        pick_kernel,
        out_shape=jax.ShapeDtypeStruct((count,) + x.shape[1:], x.dtype),
        in_specs=[pl.BlockSpec(memory_space=pltpu.SMEM), pl.BlockSpec(memory_space=pl.ANY)],
        out_specs=pl.BlockSpec(memory_space=pltpu.VMEM),
        scratch_shapes=[pltpu.SemaphoreType.DMA((count,))],
        compiler_params=pltpu.CompilerParams(vmem_limit_bytes=32 << 20),
        cost_estimate=pl.CostEstimate(flops=0, bytes_accessed=2_100_000, transcendentals=0),
        name="pick",
    )(source, x)


def homeward_kernel(owner_ref, live_ref, x_ref, out_ref):
    groups, slots, part, width = out_ref.shape
    quarter = part // SIDE
    row = lax.broadcasted_iota(jnp.int32, (part, part), 0)
    column = lax.broadcasted_iota(jnp.int32, (part, part), 1)
    order = jnp.where(column == (row % SIDE) * quarter + row // SIDE, 1.0, 0.0).astype(jnp.bfloat16)
    for g in range(groups):
        for s in range(slots):
            start = pl.multiple_of(owner_ref[g * slots + s] * part, part)
            piece = jnp.dot(order, x_ref[pl.ds(start, part), :], preferred_element_type=jnp.float32)
            keep = live_ref[g * slots + s] > 0
            out_ref[g, s] = jnp.where(keep, piece, 0.0).astype(jnp.bfloat16)


def homeward_parts(x, owner, live, groups, slots):
    rows, width = x.shape
    smem = pl.BlockSpec(memory_space=pltpu.SMEM)
    vmem = pl.BlockSpec(memory_space=pltpu.VMEM)
    return pl.pallas_call(
        homeward_kernel,
        out_shape=jax.ShapeDtypeStruct((groups, slots, rows // groups, width), x.dtype),
        in_specs=[smem, smem, vmem],
        out_specs=vmem,
        compiler_params=pltpu.CompilerParams(vmem_limit_bytes=32 << 20),
        cost_estimate=pl.CostEstimate(flops=270_000_000, bytes_accessed=3_200_000, transcendentals=0),
        name="homeward",
    )(owner, live, x)


def exchange(x, axis):
    return lax.all_to_all(x, axis, split_axis=0, concat_axis=0, tiled=True)


def body(
    home_points,
    counts,
    owner_group,
    neighbors_home,
    hilbert_target,
    neighbors_second,
    depth_first,
    mixing_first,
    gain_first,
    w_qkv_first,
    w_out_first,
    depth_second,
    mixing_second,
    gain_second,
    w_qkv_second,
    w_out_second,
):
    groups = lax.axis_size("grp")
    owners = lax.axis_size("dev")
    home_rows, width = home_points.shape
    slots = owner_group.shape[0]
    rows = home_rows // slots
    blocks = hilbert_target.shape[0]
    part = rows // groups
    side = rows // owners
    first_params = (depth_first, mixing_first, gain_first, w_qkv_first, w_out_first)
    second_params = (depth_second, mixing_second, gain_second, w_qkv_second, w_out_second)

    letters = enclosed(neighbors_home, jnp.concatenate([counts, owner_group]), slots, groups, width)
    points = jnp.concatenate([home_points.reshape(slots, groups, part, width), letters], axis=2)
    spread = exchange(jnp.transpose(points, (1, 0, 2, 3)), "grp")
    plan = spread[:, 0, part + LIST_ROWS, : 1 + slots].astype(jnp.int32)
    live = (jnp.arange(slots)[None, :] < plan[:, :1]).reshape(-1)
    owner = plan[:, 1:].reshape(-1)
    match = live[None, :] & (owner[None, :] == jnp.arange(groups)[:, None])
    source = jnp.sum(jnp.where(match, jnp.arange(groups * slots)[None, :], 0), axis=1)
    owned = exchange(pick_parts(spread.reshape((groups * slots,) + spread.shape[2:]), source), "grp")

    arrival = (neighbors_second % side) * side + neighbors_second // side
    second_lists = staged(arrival, rows)
    owned, hilbert_target = lax.optimization_barrier((owned, hilbert_target))
    targets = exchange(jnp.broadcast_to(hilbert_target[None], (owners, blocks)), "dev")
    section_one = encoder_block(owned, None, first_params, rows)
    flat = targets.reshape(-1)
    pieces = flat.shape[0]
    inverse = jnp.sum(jnp.where(flat[None, :] == jnp.arange(pieces)[:, None], jnp.arange(pieces)[None, :], 0), axis=1)
    pair = jnp.arange(2)[None, :]
    forward_rows = (2 * inverse[:, None] + pair).reshape(-1)
    by_part = jnp.transpose(targets.reshape(owners, groups, -1), (1, 0, 2)).reshape(-1, 1)
    backward_rows = (2 * by_part + pair).reshape(-1)

    mid = exchange(section_one.reshape(owners, side, width), "dev").reshape(rows, width)
    mid = permute_rows(mid, forward_rows)
    regrouped = exchange(mid.reshape(owners, side, width), "dev").reshape(rows, width)
    section_two = encoder_block(regrouped, second_lists, second_params, rows)
    mid = exchange(section_two.reshape(owners, side, width), "dev").reshape(rows, width)
    mid = permute_rows(mid, backward_rows)
    returned = exchange(mid.reshape(groups * owners, -1, width), ("grp", "dev")).reshape(rows, width)
    homeward = homeward_parts(returned, owner, live.astype(jnp.int32), groups, slots)
    delivered = exchange(homeward, "grp")
    return jnp.transpose(delivered, (1, 0, 2, 3)).reshape(home_rows, width)


def solution(mesh):
    return jax.shard_map(
        body,
        mesh=mesh,
        in_specs=(
            P(("grp", "dev"), None),
            P(("grp", "dev")),
            P(("grp", "dev")),
            P(None, ("grp", "dev")),
            P(("grp", "dev")),
            P(None, ("grp", "dev")),
            P(),
            P(),
            P(),
            P(),
            P(),
            P(),
            P(),
            P(),
            P(),
            P(),
        ),
        out_specs=P(("grp", "dev"), None),
        check_vma=False,
    )
```

time: 383 us -> 333 us (0.87)
  blocking collectives: 115 us -> 65 us
  waiting for transfers between devices: 77.7 us -> 120 us
  Pallas kernels: 108 us -> 82.9 us
  local copies, waits for them, and re-layouts: 23.8 us -> 9.68 us
    unnamed x2 -> x0, blocking collectives: 55.1 us -> none
    all_to_all x8 -> x6, waiting for transfers between devices: 77.7 us -> 120 us  [exchange(): return lax.all_to_all(x, axis, split_axis=0, concat_axis=0, tiled=True)]
    pallas_call x2 -> x4, Pallas kernels: 104 us -> 79.4 us  [the longest x2 75 us: encoder_block(): pl.pallas_call(functools.partial(block_kernel, first), out_shape=jax.Shap...]
    all_to_all x2, blocking collectives: 59.7 us -> 65 us  [exchange(): return lax.all_to_all(x, axis, split_axis=0, concat_axis=0, tiled=True)]
    gather x3 -> x0, local copies, waits for them, and re-layouts: 4.59 us -> none  [the longest x1 3.33 us: body(): owned = exchange(spread[source], 'grp').reshape(rows, width)]
    mul x3 -> x2, local copies, waits for them, and re-layouts: 4.64 us -> 0.28 us  [body(): backward_rows = (2 * by_part + pair).reshape(-1)]
    all_to_all x8 -> x6, starting transfers between devices: 53.6 us -> 50.2 us  [exchange(): return lax.all_to_all(x, axis, split_axis=0, concat_axis=0, tiled=True)]
  transfers between devices with their start and end apart: 8 -> 6, of which waited for: 6 -> 5; matrix products, arithmetic and copies ran while one was open for 4% -> 1% of each run, Pallas kernels for 0% -> 11%
where the time goes in v2:
time: 333 us; the launch traced here: 332 us
  waiting for transfers between devices  120 us (36%)
  Pallas kernels  82.9 us (25%)
  blocking collectives  65 us (20%)
  starting transfers between devices  50.2 us (15%)
  local copies, waits for them, and re-layouts  9.68 us (3%)
  other arithmetic  3.55 us (1%)
    all_to_all x6, waiting for transfers between devices, exchange(): return lax.all_to_all(x, axis, split_axis=0, concat_axis=0, tiled=True)  120 us
    pallas_call x2, Pallas kernels, encoder_block(): pl.pallas_call(functools.partial(block_kernel, first), out_shape=jax.Shap...  75 us
    all_to_all x2, blocking collectives, exchange(): return lax.all_to_all(x, axis, split_axis=0, concat_axis=0, tiled=True)  65 us
    all_to_all x6, starting transfers between devices, exchange(): return lax.all_to_all(x, axis, split_axis=0, concat_axis=0, tiled=True)  50.2 us
  transfers between devices with their start and end apart: 6, of which 5 were waited for; matrix products, arithmetic and copies ran while one was open for 1% of the time, Pallas kernels for 11%

profile of v2, /device:TPU:1, one launch (start us, length us, event | category | flops | bytes accessed | tf_op | source)
XLA Modules:
  0.0 332.1 jit_solution(11862711029946657844)
XLA Ops:
  0.0 1.3 reshape.149
  1.3 0.1 copy.80
  1.4 0.9 fusion.1
  2.3 0.3 pad_maximum_fusion
  3.3 0.7 pad_add_fusion
  4.1 0.2 maximum_bitcast_fusion
  4.3 0.2 copy.65
  4.5 35.0 %all_to_all.41 = bf16[8,2,144,512]{3,2,1,0:T(8,128)(2,1)S(1)} all-to-all(bf16[8,2,144,512]{3,2,1,0:T(8,128)(2,1)S(1)} %copy.65), channel_id=1, replica_groups=mesh['grp'=8,'dev'=32] {'grp'}, dimensions={0} | all-to-all | bytes 4718592 | tf_op jit(solution)/shard_map/all_to_all | solution.py:301
  39.5 0.1 copy.75
  39.6 0.1 copy.67
  39.7 0.1 reshape.151.owner_ref
  39.9 0.1 lt.40
  40.0 0.1 select_reduce_fusion.1.source_ref
  40.1 3.2 pick.1
  43.3 4.7 %all-to-all-start.1 = ((bf16[8,144,512]{2,1,0:T(8,128)(2,1)}), bf16[8,144,512]{2,1,0:T(8,128)(2,1)S(1)}, u32[]{:S(2)}, u32[]{:S(2)}) async-start(bf16[8,144,512]{2,1,0:T(8,128)(2,1)} %pick.1), calls=%async_computation.1 | async-start | bytes 2359296 | tf_op jit(solution)/shard_map/all_to_all | solution.py:301
  48.0 16.5 %all-to-all-done.1.refs_0_ = bf16[8,144,512]{2,1,0:T(8,128)(2,1)S(1)} async-done(((bf16[8,144,512]{2,1,0:T(8,128)(2,1)}), bf16[8,144,512]{2,1,0:T(8,128)(2,1)S(1)}, u32[]{:S(2)}, u32[]{:S(2)}) %all-to-all-start.1) | async-done | bytes 1179680 | tf_op jit(solution)/shard_map/all_to_all | solution.py:301
  64.5 0.6 broadcast_in_dim.43
  65.1 11.1 %all-to-all-start.3 = ((s32[32,1,16]{2,1,0:T(1,128)}), s32[32,1,16]{2,1,0:T(1,128)S(1)}, u32[]{:S(2)}, u32[]{:S(2)}) async-start(s32[32,1,16]{2,1,0:T(1,128)} %broadcast_in_dim.43), calls=%async_computation.3 | async-start | bytes 32768 | tf_op jit(solution)/shard_map/all_to_all | solution.py:301
  76.3 1.4 copy-done
  77.7 37.8 %block.2 = bf16[1024,512]{1,0:T(8,128)(2,1)} custom-call(bf16[8,144,512]{2,1,0:T(8,128)(2,1)S(1)} %all-to-all-done.1.refs_0_, f32[27,4,128]{2,1,0:T(4,128)S(1)} %reshape.154.refs_1_, bf16[512,512]{1,0:T(8,128)(2,1)S(1)} %copy-done.2, f32[1,512]{1,0:T(1,128)S(1)} %bitcast.36, bf16[512,1536]{1,0:T(8,128)(2,1)S(1)} %copy-done, bf16[512,512]{1,0:T(8,128)(2,1)S(1)} %copy-done.3), custom_call_target="tpu_custom_call" | custom-call | flops 5000000000 | bytes 6000000 | tf_op jit(solution)/shard_map/block/pallas_call | solution.py:187
  115.5 9.2 %all-to-all-start.2 = ((bf16[32,32,512]{2,1,0:T(8,128)(2,1)}), bf16[32,32,512]{2,1,0:T(8,128)(2,1)S(1)}, u32[]{:S(2)}, u32[]{:S(2)}) async-start(bf16[32,32,512]{2,1,0:T(8,128)(2,1)} %bitcast.8), calls=%async_computation.2 | async-start | bytes 2097152 | tf_op jit(solution)/shard_map/all_to_all | solution.py:301
  124.7 0.5 broadcast.89
  125.2 0.6 reduce.3
  125.8 0.1 eq.35
  125.9 0.2 select_reduce_fusion
  126.1 0.1 iota_add_fusion.1
  126.2 0.1 add.80.source_ref
  126.4 24.0 %all-to-all-done.2 = bf16[32,32,512]{2,1,0:T(8,128)(2,1)S(1)} async-done(((bf16[32,32,512]{2,1,0:T(8,128)(2,1)}), bf16[32,32,512]{2,1,0:T(8,128)(2,1)S(1)}, u32[]{:S(2)}, u32[]{:S(2)}) %all-to-all-start.2) | async-done | bytes 1048608 | tf_op jit(solution)/shard_map/all_to_all | solution.py:301
  150.3 2.3 permute.2
  152.6 7.0 %all-to-all-start.4 = ((bf16[32,32,512]{2,1,0:T(8,128)(2,1)}), bf16[32,32,512]{2,1,0:T(8,128)(2,1)S(1)}, u32[]{:S(2)}, u32[]{:S(2)}) async-start(bf16[32,32,512]{2,1,0:T(8,128)(2,1)} %bitcast.10), calls=%async_computation.4 | async-start | bytes 2097152 | tf_op jit(solution)/shard_map/all_to_all | solution.py:301
  159.6 0.1 fusion.4
  159.9 24.4 %all-to-all-done.4 = bf16[32,32,512]{2,1,0:T(8,128)(2,1)S(1)} async-done(((bf16[32,32,512]{2,1,0:T(8,128)(2,1)}), bf16[32,32,512]{2,1,0:T(8,128)(2,1)S(1)}, u32[]{:S(2)}, u32[]{:S(2)}) %all-to-all-start.4) | async-done | bytes 1048608 | tf_op jit(solution)/shard_map/all_to_all | solution.py:301
  184.3 1.4 copy-done.1
  185.7 37.2 %block.3 = bf16[1024,512]{1,0:T(8,128)(2,1)} custom-call(s32[8,32,128]{2,1,0:T(8,128)S(1)} %pad.14.refs_0_, bf16[1024,512]{1,0:T(8,128)(2,1)S(1)} %bitcast.35, f32[27,4,128]{2,1,0:T(4,128)S(1)} %reshape.160.refs_2_, bf16[512,512]{1,0:T(8,128)(2,1)S(1)} %copy-done.4, f32[1,512]{1,0:T(1,128)S(1)} %bitcast.37, bf16[512,1536]{1,0:T(8,128)(2,1)S(1)} %copy-done.1, ...), custom_call_target="tpu_custom_call" | custom-call | flops 5000000000 | bytes 6000000 | tf_op jit(solution)/shard_map/block/pallas_call | solution.py:187
  222.9 7.2 %all-to-all-start.5 = ((bf16[32,32,512]{2,1,0:T(8,128)(2,1)}), bf16[32,32,512]{2,1,0:T(8,128)(2,1)S(1)}, u32[]{:S(2)}, u32[]{:S(2)}) async-start(bf16[32,32,512]{2,1,0:T(8,128)(2,1)} %bitcast.13), calls=%async_computation.5 | async-start | bytes 2097152 | tf_op jit(solution)/shard_map/all_to_all | solution.py:301
  230.2 0.1 copy.71
  230.3 0.1 mul.42
  230.4 0.1 iota_add_fusion
  230.6 0.1 add.81.source_ref
  230.7 23.7 %all-to-all-done.5 = bf16[32,32,512]{2,1,0:T(8,128)(2,1)S(1)} async-done(((bf16[32,32,512]{2,1,0:T(8,128)(2,1)}), bf16[32,32,512]{2,1,0:T(8,128)(2,1)S(1)}, u32[]{:S(2)}, u32[]{:S(2)}) %all-to-all-start.5) | async-done | bytes 1048608 | tf_op jit(solution)/shard_map/all_to_all | solution.py:301
  254.5 1.3 permute.3
  255.8 1.1 reshape.164
  256.9 11.0 %all-to-all-start.6 = ((bf16[256,4,512]{2,1,0:T(4,128)(2,1)}), bf16[256,4,512]{2,1,0:T(4,128)(2,1)S(1)}, u32[]{:S(2)}, u32[]{:S(2)}) async-start(bf16[256,4,512]{2,1,0:T(4,128)(2,1)} %reshape.164), calls=%async_computation.6 | async-start | bytes 2097152 | tf_op jit(solution)/shard_map/all_to_all | solution.py:301
  267.9 31.2 %all-to-all-done.6 = bf16[256,4,512]{2,1,0:T(4,128)(2,1)S(1)} async-done(((bf16[256,4,512]{2,1,0:T(4,128)(2,1)}), bf16[256,4,512]{2,1,0:T(4,128)(2,1)S(1)}, u32[]{:S(2)}, u32[]{:S(2)}) %all-to-all-start.6) | async-done | bytes 1048608 | tf_op jit(solution)/shard_map/all_to_all | solution.py:301
  299.1 0.3 reshape.165.x_ref
  299.3 1.2 homeward.1
  300.6 30.0 %all_to_all.42 = bf16[8,2,128,512]{3,2,1,0:T(8,128)(2,1)S(1)} all-to-all(bf16[8,2,128,512]{3,2,1,0:T(8,128)(2,1)S(1)} %homeward.1), channel_id=1, replica_groups=mesh['grp'=8,'dev'=32] {'grp'}, dimensions={0} | all-to-all | bytes 4194304 | tf_op jit(solution)/shard_map/all_to_all | solution.py:301
  330.6 1.5 copy.73
  (44 shorter events, 0.4 us)
Async XLA Ops:
  0.0 4.1 %copy-start.8 = (bf16[2048,512]{1,0:T(8,128)(2,1)S(1)}, bf16[2048,512]{1,0:T(8,128)(2,1)}, u32[]{:S(2)}) copy-start(bf16[2048,512]{1,0:T(8,128)(2,1)} %param.16) | copy-start | bytes 6291460
  40.1 7.9 %copy-start.10 = (f32[27,512]{1,0:T(8,128)S(1)}, f32[27,512]{1,0:T(8,128)}, u32[]{:S(2)}) copy-start(f32[27,512]{1,0:T(8,128)} %param.22) | copy-start | bytes 165892
  40.1 24.4 %copy-start.12 = (s32[16]{0:T(128)S(1)}, s32[16]{0:T(128)}, u32[]{:S(2)}) copy-start(s32[16]{0:T(128)} %param.20) | copy-start | bytes 196
  40.1 36.1 %copy-start.2 = (bf16[512,512]{1,0:T(8,128)(2,1)S(1)}, bf16[512,512]{1,0:T(8,128)(2,1)}, u32[]{:S(2)}) copy-start(bf16[512,512]{1,0:T(8,128)(2,1)} %refs_2_.1) | copy-start | bytes 1572868
  40.1 36.1 %copy-start.6 = (f32[512]{0:T(512)S(1)}, f32[512]{0:T(512)}, u32[]{:S(2)}) copy-start(f32[512]{0:T(512)} %param.24) | copy-start | bytes 6148
  43.3 33.0 %copy-start.3 = (bf16[512,512]{1,0:T(8,128)(2,1)S(1)}, bf16[512,512]{1,0:T(8,128)(2,1)}, u32[]{:S(2)}) copy-start(bf16[512,512]{1,0:T(8,128)(2,1)} %refs_5_.2) | copy-start | bytes 1572868
  43.3 21.2 %all-to-all-start.1 = ((bf16[8,144,512]{2,1,0:T(8,128)(2,1)}), bf16[8,144,512]{2,1,0:T(8,128)(2,1)S(1)}, u32[]{:S(2)}, u32[]{:S(2)}) async-start(bf16[8,144,512]{2,1,0:T(8,128)(2,1)} %pick.1), calls=%async_computation.1 | async-start | bytes 2359296 | tf_op jit(solution)/shard_map/all_to_all | solution.py:301
  65.1 50.4 %all-to-all-start.3 = ((s32[32,1,16]{2,1,0:T(1,128)}), s32[32,1,16]{2,1,0:T(1,128)S(1)}, u32[]{:S(2)}, u32[]{:S(2)}) async-start(s32[32,1,16]{2,1,0:T(1,128)} %broadcast_in_dim.43), calls=%async_computation.3 | async-start | bytes 32768 | tf_op jit(solution)/shard_map/all_to_all | solution.py:301
  76.3 1.4 copy-start
  115.5 34.8 %all-to-all-start.2 = ((bf16[32,32,512]{2,1,0:T(8,128)(2,1)}), bf16[32,32,512]{2,1,0:T(8,128)(2,1)S(1)}, u32[]{:S(2)}, u32[]{:S(2)}) async-start(bf16[32,32,512]{2,1,0:T(8,128)(2,1)} %bitcast.8), calls=%async_computation.2 | async-start | bytes 2097152 | tf_op jit(solution)/shard_map/all_to_all | solution.py:301
  150.3 9.3 %copy-start.9 = (s32[27,1024]{1,0:T(8,128)S(1)}, s32[27,1024]{1,0:T(8,128)}, u32[]{:S(2)}) copy-start(s32[27,1024]{1,0:T(8,128)} %param.21) | copy-start | bytes 331780
  152.6 7.3 %copy-start.11 = (f32[27,512]{1,0:T(8,128)S(1)}, f32[27,512]{1,0:T(8,128)}, u32[]{:S(2)}) copy-start(f32[27,512]{1,0:T(8,128)} %param.27) | copy-start | bytes 165892
  152.6 31.7 %copy-start.4 = (bf16[512,512]{1,0:T(8,128)(2,1)S(1)}, bf16[512,512]{1,0:T(8,128)(2,1)}, u32[]{:S(2)}) copy-start(bf16[512,512]{1,0:T(8,128)(2,1)} %refs_3_.1) | copy-start | bytes 1572868
  152.6 31.7 %copy-start.5 = (bf16[512,512]{1,0:T(8,128)(2,1)S(1)}, bf16[512,512]{1,0:T(8,128)(2,1)}, u32[]{:S(2)}) copy-start(bf16[512,512]{1,0:T(8,128)(2,1)} %refs_6_.1) | copy-start | bytes 1572868
  152.6 31.7 %copy-start.7 = (f32[512]{0:T(512)S(1)}, f32[512]{0:T(512)}, u32[]{:S(2)}) copy-start(f32[512]{0:T(512)} %param.29) | copy-start | bytes 6148
  152.6 31.6 %all-to-all-start.4 = ((bf16[32,32,512]{2,1,0:T(8,128)(2,1)}), bf16[32,32,512]{2,1,0:T(8,128)(2,1)S(1)}, u32[]{:S(2)}, u32[]{:S(2)}) async-start(bf16[32,32,512]{2,1,0:T(8,128)(2,1)} %bitcast.10), calls=%async_computation.4 | async-start | bytes 2097152 | tf_op jit(solution)/shard_map/all_to_all | solution.py:301
  184.3 1.4 copy-start.1
  222.9 31.6 %all-to-all-start.5 = ((bf16[32,32,512]{2,1,0:T(8,128)(2,1)}), bf16[32,32,512]{2,1,0:T(8,128)(2,1)S(1)}, u32[]{:S(2)}, u32[]{:S(2)}) async-start(bf16[32,32,512]{2,1,0:T(8,128)(2,1)} %bitcast.13), calls=%async_computation.5 | async-start | bytes 2097152 | tf_op jit(solution)/shard_map/all_to_all | solution.py:301
  256.9 42.2 %all-to-all-start.6 = ((bf16[256,4,512]{2,1,0:T(4,128)(2,1)}), bf16[256,4,512]{2,1,0:T(4,128)(2,1)S(1)}, u32[]{:S(2)}, u32[]{:S(2)}) async-start(bf16[256,4,512]{2,1,0:T(4,128)(2,1)} %reshape.164), calls=%async_computation.6 | async-start | bytes 2097152 | tf_op jit(solution)/shard_map/all_to_all | solution.py:301

commit v3 on v2

--- a/solution.py
+++ b/solution.py
@@ -16,21 +16,22 @@
 CHUNK = 128
 BUFFERS = 2
 LIST_ROWS = 14
+NOTE_ROWS = 8
 
 
 def block_kernel(first, *refs):
     if first:
         (
-            x_ref, depth_ref, mixing_ref, gain_ref, w_qkv_ref, w_out_ref, out_ref,
-            plain, summed, updated, project, mixed, scores_even, scores_odd, lists_ref, *stage
+            x_ref, note_ref, depth_ref, mixing_ref, gain_ref, w_qkv_ref, w_out_ref, out_ref,
+            plain, summed, updated, project, mixed, scores_even, scores_odd, powers_even, powers_odd, lists_ref, *stage
         ) = refs
     else:
         (
             lists_ref, x_ref, depth_ref, mixing_ref, gain_ref, w_qkv_ref, w_out_ref, out_ref,
-            plain, summed, updated, project, mixed, scores_even, scores_odd, *stage
+            plain, summed, updated, project, mixed, scores_even, scores_odd, powers_even, powers_odd, *stage
         ) = refs
     buffers, sems = stage[:BUFFERS], stage[BUFFERS]
-    rows, width = out_ref.shape
+    rows, width = updated.shape
     fanout = depth_ref.shape[0]
     chunks = width // LANES
     pairs = width // LANES
@@ -142,51 +143,69 @@
         keys = project[:, pl.ds(width + col0, LANES)]
         target[...] = lax.dot_general(own, keys, (((1,), (1,)), ((), ())), preferred_element_type=jnp.float32)
 
-    def weigh(step, source):
+    def weigh(source, target):
+        scores = source[...]
+        peak = jnp.max(scores, axis=-1, keepdims=True)
+        target[...] = jnp.exp2(scores - peak).astype(jnp.bfloat16)
+
+    def blend(step, half, source):
         row0, col0 = place(step)
-        scores = source[...]
         values = jnp.concatenate([project[:, pl.ds(2 * width + col0, LANES)], ones], axis=1)
-        peak = jnp.max(scores, axis=-1, keepdims=True)
-        powers = jnp.exp2(scores - peak).astype(jnp.bfloat16)
-        both = jnp.dot(powers, values, preferred_element_type=jnp.float32)
-        return both[:, :LANES] / both[:, LANES:]
-
+        both = jnp.dot(source[...], values, preferred_element_type=jnp.float32)
+        result = (both[:, :LANES] / both[:, LANES:]).astype(jnp.bfloat16)
+        keep = left if half == 0 else jnp.logical_not(left)
+        spot = (pl.ds(row0, TILE), pl.ds(col0, LANES))
+        mixed[spot] = jnp.where(keep, result, mixed[spot])
+
+    last = pairs * tiles - 1
     score(0, 0, scores_even)
+    powers_odd[...] = jnp.ones_like(powers_odd)
 
     def attend(step, carry):
-        row0, col0 = place(step)
         score(step, 1, scores_odd)
-        left_result = weigh(step, scores_even)
-        score(jnp.minimum(step + 1, pairs * tiles - 1), 0, scores_even)
-        right_result = weigh(step, scores_odd)
-        mixed[pl.ds(row0, TILE), pl.ds(col0, LANES)] = jnp.where(left, left_result, right_result).astype(jnp.bfloat16)
+        weigh(scores_even, powers_even)
+        blend(jnp.maximum(step - 1, 0), 1, powers_odd)
+        score(jnp.minimum(step + 1, last), 0, scores_even)
+        weigh(scores_odd, powers_odd)
+        blend(step, 0, powers_even)
         return carry
 
     lax.fori_loop(0, pairs * tiles, attend, 0)
+    blend(last, 1, powers_odd)
 
     def tail(tile, carry):
         row0 = pl.multiple_of(tile * TILE, TILE)
-        out_ref[pl.ds(row0, TILE), :] = (
+        result = (
             updated[pl.ds(row0, TILE), :]
             + jnp.dot(mixed[pl.ds(row0, TILE), :], w_out_ref[...], preferred_element_type=jnp.float32)
         ).astype(jnp.bfloat16)
+        if first:
+            for i in range(TILE // SIDE):
+                for c in range(chunks):
+                    out_ref[tile * (TILE // SIDE) + i, c * SIDE : (c + 1) * SIDE, :] = result[
+                        i * SIDE : (i + 1) * SIDE, c * LANES : (c + 1) * LANES
+                    ]
+        else:
+            out_ref[pl.ds(row0, TILE), :] = result
         return carry
 
     lax.fori_loop(0, tiles, tail, 0)
-
-
-def encoder_block(features, lists, params, rows):
+    if first:
+        for i in range(rows // SIDE):
+            out_ref[i, chunks * SIDE :, :] = note_ref[...]
+
+
+def encoder_block(features, beside, params, rows, first):
     depth, mixing, gain, w_qkv, w_out = params
     fanout, width = depth.shape
-    first = lists is None
     vmem = pl.BlockSpec(memory_space=pltpu.VMEM)
     table = (rows // CHUNK, SIDE, LANES)
-    operands = (features, depth.reshape(fanout, -1, LANES), mixing, gain.reshape(1, width), w_qkv, w_out)
-    if not first:
-        operands = (lists,) + operands
+    operands = (depth.reshape(fanout, -1, LANES), mixing, gain.reshape(1, width), w_qkv, w_out)
+    operands = ((features, beside) if first else (beside, features)) + operands
+    shape = (rows // SIDE, SIDE * width // LANES + NOTE_ROWS, LANES) if first else (rows, width)
     return pl.pallas_call(
         functools.partial(block_kernel, first),
-        out_shape=jax.ShapeDtypeStruct((rows, width), jnp.bfloat16),
+        out_shape=jax.ShapeDtypeStruct(shape, jnp.bfloat16),
         in_specs=[vmem] * len(operands),
         out_specs=vmem,
         scratch_shapes=[
@@ -197,6 +216,8 @@
             pltpu.VMEM((rows, width), jnp.bfloat16),
             pltpu.VMEM((TILE, rows), jnp.float32),
             pltpu.VMEM((TILE, rows), jnp.float32),
+            pltpu.VMEM((TILE, rows), jnp.bfloat16),
+            pltpu.VMEM((TILE, rows), jnp.bfloat16),
         ]
         + [pltpu.VMEM(table, jnp.int32)] * first
         + [pltpu.SMEM(table[1:], jnp.int32)] * BUFFERS
@@ -242,6 +263,43 @@
         cost_estimate=pl.CostEstimate(flops=1_100_000_000, bytes_accessed=2_100_000, transcendentals=0),
         name="permute",
     )(x, source.reshape(-1, 1))
+
+
+def regroup_kernel(x_ref, out_ref, places_ref, joined):
+    pieces = x_ref.shape[0]
+    rows, width = joined.shape
+    body = SIDE * width // LANES
+    for i in range(pieces):
+        for c in range(width // LANES):
+            joined[i * SIDE : (i + 1) * SIDE, c * LANES : (c + 1) * LANES] = x_ref[i, c * SIDE : (c + 1) * SIDE, :]
+    high, low = [], []
+    for i in range(0, pieces, LANES // SIDE):
+        notes = [x_ref[i + k, body:, :].astype(jnp.float32) for k in range(LANES // SIDE)]
+        note = functools.reduce(jnp.add, notes)
+        high.append(note[0:1, :])
+        low.append(note[1:2, :])
+    places = (jnp.concatenate(high, axis=1) * 32.0 + jnp.concatenate(low, axis=1)).astype(jnp.int32)
+    places_ref[...] = jnp.broadcast_to(places, places_ref.shape)
+    for tile in range(rows // TILE):
+        own = lax.broadcasted_iota(jnp.int32, (TILE, rows), 0) + tile * TILE
+        chosen = jnp.where(own == places, 1.0, 0.0).astype(jnp.bfloat16)
+        out_ref[tile * TILE : (tile + 1) * TILE, :] = jnp.dot(
+            chosen, joined[...], preferred_element_type=jnp.float32
+        ).astype(jnp.bfloat16)
+
+
+def regroup_rows(x, rows, width):
+    vmem = pl.BlockSpec(memory_space=pltpu.VMEM)
+    return pl.pallas_call(
+        regroup_kernel,
+        out_shape=(jax.ShapeDtypeStruct((rows, width), x.dtype), jax.ShapeDtypeStruct((8, rows), jnp.int32)),
+        in_specs=[vmem],
+        out_specs=(vmem, vmem),
+        scratch_shapes=[pltpu.VMEM((rows, width), jnp.bfloat16)],
+        compiler_params=pltpu.CompilerParams(vmem_limit_bytes=32 << 20),
+        cost_estimate=pl.CostEstimate(flops=1_100_000_000, bytes_accessed=2_200_000, transcendentals=0),
+        name="regroup",
+    )(x)
 
 
 def pick_kernel(source_ref, x_ref, out_ref, sems):
@@ -342,21 +400,20 @@
 
     arrival = (neighbors_second % side) * side + neighbors_second // side
     second_lists = staged(arrival, rows)
-    owned, hilbert_target = lax.optimization_barrier((owned, hilbert_target))
-    targets = exchange(jnp.broadcast_to(hilbert_target[None], (owners, blocks)), "dev")
-    section_one = encoder_block(owned, None, first_params, rows)
-    flat = targets.reshape(-1)
-    pieces = flat.shape[0]
-    inverse = jnp.sum(jnp.where(flat[None, :] == jnp.arange(pieces)[:, None], jnp.arange(pieces)[None, :], 0), axis=1)
+    column = lax.axis_index("dev")
     pair = jnp.arange(2)[None, :]
-    forward_rows = (2 * inverse[:, None] + pair).reshape(-1)
+    places = (2 * hilbert_target[:, None] + pair).reshape(1, -1)
+    digits = jnp.concatenate([places // 32, places % 32, jnp.zeros((NOTE_ROWS - 2, side), jnp.int32)])
+    mine = jnp.arange(LANES // side) == column % (LANES // side)
+    note = jnp.where(mine[None, :, None], digits[:, None, :], 0).reshape(NOTE_ROWS, LANES).astype(jnp.bfloat16)
+
+    section_one = encoder_block(owned, note, first_params, rows, True)
+    mid, places = regroup_rows(exchange(section_one, "dev"), rows, width)
+    targets = places[0].reshape(owners, blocks, 2)[:, :, 0] // 2
     by_part = jnp.transpose(targets.reshape(owners, groups, -1), (1, 0, 2)).reshape(-1, 1)
     backward_rows = (2 * by_part + pair).reshape(-1)
-
-    mid = exchange(section_one.reshape(owners, side, width), "dev").reshape(rows, width)
-    mid = permute_rows(mid, forward_rows)
     regrouped = exchange(mid.reshape(owners, side, width), "dev").reshape(rows, width)
-    section_two = encoder_block(regrouped, second_lists, second_params, rows)
+    section_two = encoder_block(regrouped, second_lists, second_params, rows, False)
     mid = exchange(section_two.reshape(owners, side, width), "dev").reshape(rows, width)
     mid = permute_rows(mid, backward_rows)
     returned = exchange(mid.reshape(groups * owners, -1, width), ("grp", "dev")).reshape(rows, width)

time: 333 us -> 321 us (0.964)
  blocking collectives: 65 us -> 106 us
  waiting for transfers between devices: 120 us -> 95.6 us
  starting transfers between devices: 50.2 us -> 27.4 us
  Pallas kernels: 82.9 us -> 79.1 us
    all_to_all x2 -> x3, blocking collectives: 65 us -> 106 us  [exchange(): return lax.all_to_all(x, axis, split_axis=0, concat_axis=0, tiled=True)]
    all_to_all x6 -> x4, waiting for transfers between devices: 120 us -> 95.6 us  [exchange(): return lax.all_to_all(x, axis, split_axis=0, concat_axis=0, tiled=True)]
    all_to_all x6 -> x4, starting transfers between devices: 50.2 us -> 27.4 us  [exchange(): return lax.all_to_all(x, axis, split_axis=0, concat_axis=0, tiled=True)]
    pallas_call x2, Pallas kernels: 75 us -> 71.1 us  [encoder_block(): pl.pallas_call(functools.partial(block_kernel, first), out_shape=jax.Shap...]
  transfers between devices with their start and end apart: 6 -> 4, of which waited for: 5 -> 4; matrix products, arithmetic and copies ran while one was open for 1% -> 1% of each run, Pallas kernels for 11% -> 0%
where the time goes in v3:
time: 321 us
  blocking collectives  106 us (33%)
  waiting for transfers between devices  95.6 us (30%)
  Pallas kernels  79.1 us (25%)
  starting transfers between devices  27.4 us (9%)
  local copies, waits for them, and re-layouts  8.95 us (3%)
    all_to_all x3, blocking collectives, exchange(): return lax.all_to_all(x, axis, split_axis=0, concat_axis=0, tiled=True)  106 us
    all_to_all x4, waiting for transfers between devices, exchange(): return lax.all_to_all(x, axis, split_axis=0, concat_axis=0, tiled=True)  95.6 us
    pallas_call x2, Pallas kernels, encoder_block(): pl.pallas_call(functools.partial(block_kernel, first), out_shape=jax.Shap...  71.1 us
    all_to_all x4, starting transfers between devices, exchange(): return lax.all_to_all(x, axis, split_axis=0, concat_axis=0, tiled=True)  27.4 us
  transfers between devices with their start and end apart: 4, of which 4 were waited for; matrix products, arithmetic and copies ran while one was open for 1% of the time, Pallas kernels for 0%

profile of v3, /device:TPU:1, one launch (start us, length us, event | category | flops | bytes accessed | tf_op | source)
XLA Modules:
  0.0 320.8 jit_solution(16081959565787780414)
XLA Ops:
  0.8 0.7 pad_add_fusion
  1.5 1.1 reshape.268
  2.7 0.1 copy.75
  2.8 0.9 fusion.1
  3.7 0.3 pad_maximum_fusion
  4.1 0.2 maximum_bitcast_fusion
  4.3 0.2 copy.61
  4.5 35.0 %all_to_all.35 = bf16[8,2,144,512]{3,2,1,0:T(8,128)(2,1)S(1)} all-to-all(bf16[8,2,144,512]{3,2,1,0:T(8,128)(2,1)S(1)} %copy.61), channel_id=1, replica_groups=mesh['grp'=8,'dev'=32] {'grp'}, dimensions={0} | all-to-all | bytes 4718592 | tf_op jit(solution)/shard_map/all_to_all | solution.py:359
  39.5 0.1 copy.70
  39.6 0.1 copy.63
  39.7 0.1 reshape.270.owner_ref
  39.8 0.1 iota_compare_fusion.1
  39.9 0.1 lt.52
  40.0 0.1 select_reduce_fusion.source_ref
  40.1 3.2 pick.1
  43.3 4.7 %all-to-all-start.1 = ((bf16[8,144,512]{2,1,0:T(8,128)(2,1)}), bf16[8,144,512]{2,1,0:T(8,128)(2,1)S(1)}, u32[]{:S(2)}, u32[]{:S(2)}) async-start(bf16[8,144,512]{2,1,0:T(8,128)(2,1)} %pick.1), calls=%async_computation.1 | async-start | bytes 2359296 | tf_op jit(solution)/shard_map/all_to_all | solution.py:359
  48.0 0.1 iota_add_fusion.1
  48.1 0.1 add.123
  48.2 0.1 pad.17.clone
  48.3 0.1 broadcast_in_dim.59
  48.4 0.1 broadcast_in_dim.54
  48.5 0.1 broadcast_in_dim.55
  48.6 15.9 %all-to-all-done.1.refs_0_ = bf16[8,144,512]{2,1,0:T(8,128)(2,1)S(1)} async-done(((bf16[8,144,512]{2,1,0:T(8,128)(2,1)}), bf16[8,144,512]{2,1,0:T(8,128)(2,1)S(1)}, u32[]{:S(2)}, u32[]{:S(2)}) %all-to-all-start.1) | async-done | bytes 1179680 | tf_op jit(solution)/shard_map/all_to_all | solution.py:359
  64.5 1.4 copy-done
  65.9 35.4 %block.2 = bf16[32,136,128]{2,1,0:T(8,128)(2,1)S(1)} custom-call(bf16[8,144,512]{2,1,0:T(8,128)(2,1)S(1)} %all-to-all-done.1.refs_0_, bf16[8,128]{1,0:T(8,128)(2,1)S(1)} %select_convert_fusion.refs_1_, f32[27,4,128]{2,1,0:T(4,128)S(1)} %reshape.273.refs_2_, bf16[512,512]{1,0:T(8,128)(2,1)S(1)} %copy-done.2, f32[1,512]{1,0:T(1,128)S(1)} %bitcast.34, ...), custom_call_target="tpu_custom_call" | custom-call | flops 5000000000 | bytes 6000000 | tf_op jit(solution)/shard_map/block/pallas_call | solution.py:206
  101.3 40.7 %all_to_all.36.x_ref = bf16[32,136,128]{2,1,0:T(8,128)(2,1)S(1)} all-to-all(bf16[32,136,128]{2,1,0:T(8,128)(2,1)S(1)} %block.2), channel_id=1, replica_groups=mesh['grp'=8,'dev'=32] {'dev'}, dimensions={0} | all-to-all | bytes 2228224 | tf_op jit(solution)/shard_map/all_to_all | solution.py:359
  142.0 2.3 regroup.1
  144.3 5.2 %all-to-all-start.3 = ((bf16[32,32,512]{2,1,0:T(8,128)(2,1)}), bf16[32,32,512]{2,1,0:T(8,128)(2,1)S(1)}, u32[]{:S(2)}, u32[]{:S(2)}) async-start(bf16[32,32,512]{2,1,0:T(8,128)(2,1)} %bitcast.8), calls=%async_computation.3 | async-start | bytes 2097152 | tf_op jit(solution)/shard_map/all_to_all | solution.py:359
  149.5 0.1 fusion.4
  149.8 25.0 %all-to-all-done.3 = bf16[32,32,512]{2,1,0:T(8,128)(2,1)S(1)} async-done(((bf16[32,32,512]{2,1,0:T(8,128)(2,1)}), bf16[32,32,512]{2,1,0:T(8,128)(2,1)S(1)}, u32[]{:S(2)}, u32[]{:S(2)}) %all-to-all-start.3) | async-done | bytes 1048608 | tf_op jit(solution)/shard_map/all_to_all | solution.py:359
  174.8 1.4 copy-done.1
  176.2 35.7 %block.3 = bf16[1024,512]{1,0:T(8,128)(2,1)} custom-call(s32[8,32,128]{2,1,0:T(8,128)S(1)} %pad.14.refs_0_, bf16[1024,512]{1,0:T(8,128)(2,1)S(1)} %bitcast.33, f32[27,4,128]{2,1,0:T(4,128)S(1)} %reshape.277.refs_2_, bf16[512,512]{1,0:T(8,128)(2,1)S(1)} %copy-done.4, f32[1,512]{1,0:T(1,128)S(1)} %bitcast.35, bf16[512,1536]{1,0:T(8,128)(2,1)S(1)} %copy-done.1, ...), custom_call_target="tpu_custom_call" | custom-call | flops 5000000000 | bytes 6000000 | tf_op jit(solution)/shard_map/block/pallas_call | solution.py:206
  212.0 6.7 %all-to-all-start.4 = ((bf16[32,32,512]{2,1,0:T(8,128)(2,1)}), bf16[32,32,512]{2,1,0:T(8,128)(2,1)S(1)}, u32[]{:S(2)}, u32[]{:S(2)}) async-start(bf16[32,32,512]{2,1,0:T(8,128)(2,1)} %bitcast.11), calls=%async_computation.4 | async-start | bytes 2097152 | tf_op jit(solution)/shard_map/all_to_all | solution.py:359
  218.7 0.2 reshape_squeeze.3
  218.9 0.2 copy.65
  219.2 0.1 copy.66
  219.3 0.1 mul.38
  219.4 0.1 iota_add_fusion
  219.6 0.1 add.129.source_ref
  219.7 23.6 %all-to-all-done.4 = bf16[32,32,512]{2,1,0:T(8,128)(2,1)S(1)} async-done(((bf16[32,32,512]{2,1,0:T(8,128)(2,1)}), bf16[32,32,512]{2,1,0:T(8,128)(2,1)S(1)}, u32[]{:S(2)}, u32[]{:S(2)}) %all-to-all-start.4) | async-done | bytes 1048608 | tf_op jit(solution)/shard_map/all_to_all | solution.py:359
  243.3 1.3 permute.1
  244.6 1.1 reshape.281
  245.7 10.8 %all-to-all-start.5 = ((bf16[256,4,512]{2,1,0:T(4,128)(2,1)}), bf16[256,4,512]{2,1,0:T(4,128)(2,1)S(1)}, u32[]{:S(2)}, u32[]{:S(2)}) async-start(bf16[256,4,512]{2,1,0:T(4,128)(2,1)} %reshape.281), calls=%async_computation.5 | async-start | bytes 2097152 | tf_op jit(solution)/shard_map/all_to_all | solution.py:359
  256.5 31.2 %all-to-all-done.5 = bf16[256,4,512]{2,1,0:T(4,128)(2,1)S(1)} async-done(((bf16[256,4,512]{2,1,0:T(4,128)(2,1)}), bf16[256,4,512]{2,1,0:T(4,128)(2,1)S(1)}, u32[]{:S(2)}, u32[]{:S(2)}) %all-to-all-start.5) | async-done | bytes 1048608 | tf_op jit(solution)/shard_map/all_to_all | solution.py:359
  287.7 0.3 reshape.282.x_ref
  288.0 1.2 homeward.1
  289.2 30.0 %all_to_all.37 = bf16[8,2,128,512]{3,2,1,0:T(8,128)(2,1)S(1)} all-to-all(bf16[8,2,128,512]{3,2,1,0:T(8,128)(2,1)S(1)} %homeward.1), channel_id=1, replica_groups=mesh['grp'=8,'dev'=32] {'grp'}, dimensions={0} | all-to-all | bytes 4194304 | tf_op jit(solution)/shard_map/all_to_all | solution.py:359
  319.2 1.5 copy.68
  (48 shorter events, 0.4 us)
Async XLA Ops:
  0.0 4.1 %copy-start.8 = (bf16[2048,512]{1,0:T(8,128)(2,1)S(1)}, bf16[2048,512]{1,0:T(8,128)(2,1)}, u32[]{:S(2)}) copy-start(bf16[2048,512]{1,0:T(8,128)(2,1)} %param.16) | copy-start | bytes 6291460
  40.1 7.9 %copy-start.12 = (s32[16]{0:T(128)S(1)}, s32[16]{0:T(128)}, u32[]{:S(2)}) copy-start(s32[16]{0:T(128)} %param.20) | copy-start | bytes 196
  40.1 8.5 %copy-start.10 = (f32[27,512]{1,0:T(8,128)S(1)}, f32[27,512]{1,0:T(8,128)}, u32[]{:S(2)}) copy-start(f32[27,512]{1,0:T(8,128)} %param.22) | copy-start | bytes 165892
  40.1 24.4 %copy-start.2 = (bf16[512,512]{1,0:T(8,128)(2,1)S(1)}, bf16[512,512]{1,0:T(8,128)(2,1)}, u32[]{:S(2)}) copy-start(bf16[512,512]{1,0:T(8,128)(2,1)} %refs_3_.2) | copy-start | bytes 1572868
  40.1 24.4 %copy-start.6 = (f32[512]{0:T(512)S(1)}, f32[512]{0:T(512)}, u32[]{:S(2)}) copy-start(f32[512]{0:T(512)} %param.24) | copy-start | bytes 6148
  43.3 21.2 %copy-start.3 = (bf16[512,512]{1,0:T(8,128)(2,1)S(1)}, bf16[512,512]{1,0:T(8,128)(2,1)}, u32[]{:S(2)}) copy-start(bf16[512,512]{1,0:T(8,128)(2,1)} %refs_6_.2) | copy-start | bytes 1572868
  43.3 21.2 %all-to-all-start.1 = ((bf16[8,144,512]{2,1,0:T(8,128)(2,1)}), bf16[8,144,512]{2,1,0:T(8,128)(2,1)S(1)}, u32[]{:S(2)}, u32[]{:S(2)}) async-start(bf16[8,144,512]{2,1,0:T(8,128)(2,1)} %pick.1), calls=%async_computation.1 | async-start | bytes 2359296 | tf_op jit(solution)/shard_map/all_to_all | solution.py:359
  64.5 1.4 copy-start
  142.0 7.5 %copy-start.9 = (s32[27,1024]{1,0:T(8,128)S(1)}, s32[27,1024]{1,0:T(8,128)}, u32[]{:S(2)}) copy-start(s32[27,1024]{1,0:T(8,128)} %param.21) | copy-start | bytes 331780
  144.3 5.4 %copy-start.11 = (f32[27,512]{1,0:T(8,128)S(1)}, f32[27,512]{1,0:T(8,128)}, u32[]{:S(2)}) copy-start(f32[27,512]{1,0:T(8,128)} %param.27) | copy-start | bytes 165892
  144.3 30.5 %copy-start.4 = (bf16[512,512]{1,0:T(8,128)(2,1)S(1)}, bf16[512,512]{1,0:T(8,128)(2,1)}, u32[]{:S(2)}) copy-start(bf16[512,512]{1,0:T(8,128)(2,1)} %refs_3_.3) | copy-start | bytes 1572868
  144.3 30.5 %copy-start.5 = (bf16[512,512]{1,0:T(8,128)(2,1)S(1)}, bf16[512,512]{1,0:T(8,128)(2,1)}, u32[]{:S(2)}) copy-start(bf16[512,512]{1,0:T(8,128)(2,1)} %refs_6_.3) | copy-start | bytes 1572868
  144.3 30.5 %copy-start.7 = (f32[512]{0:T(512)S(1)}, f32[512]{0:T(512)}, u32[]{:S(2)}) copy-start(f32[512]{0:T(512)} %param.29) | copy-start | bytes 6148
  144.3 30.5 %all-to-all-start.3 = ((bf16[32,32,512]{2,1,0:T(8,128)(2,1)}), bf16[32,32,512]{2,1,0:T(8,128)(2,1)S(1)}, u32[]{:S(2)}, u32[]{:S(2)}) async-start(bf16[32,32,512]{2,1,0:T(8,128)(2,1)} %bitcast.8), calls=%async_computation.3 | async-start | bytes 2097152 | tf_op jit(solution)/shard_map/all_to_all | solution.py:359
  174.8 1.4 copy-start.1
  212.0 31.3 %all-to-all-start.4 = ((bf16[32,32,512]{2,1,0:T(8,128)(2,1)}), bf16[32,32,512]{2,1,0:T(8,128)(2,1)S(1)}, u32[]{:S(2)}, u32[]{:S(2)}) async-start(bf16[32,32,512]{2,1,0:T(8,128)(2,1)} %bitcast.11), calls=%async_computation.4 | async-start | bytes 2097152 | tf_op jit(solution)/shard_map/all_to_all | solution.py:359
  245.7 42.0 %all-to-all-start.5 = ((bf16[256,4,512]{2,1,0:T(4,128)(2,1)}), bf16[256,4,512]{2,1,0:T(4,128)(2,1)S(1)}, u32[]{:S(2)}, u32[]{:S(2)}) async-start(bf16[256,4,512]{2,1,0:T(4,128)(2,1)} %reshape.281), calls=%async_computation.5 | async-start | bytes 2097152 | tf_op jit(solution)/shard_map/all_to_all | solution.py:359

commit v4 on v3

--- a/solution.py
+++ b/solution.py
@@ -11,7 +11,7 @@
 epsilon = 1e-05
 SCALE = HEAD_DIM ** (-0.5) * 1.4426950408889634
 LANES = 128
-TILE = 256
+TILE = 512
 SIDE = 32
 CHUNK = 128
 BUFFERS = 2
@@ -222,7 +222,7 @@
         + [pltpu.VMEM(table, jnp.int32)] * first
         + [pltpu.SMEM(table[1:], jnp.int32)] * BUFFERS
         + [pltpu.SemaphoreType.DMA((BUFFERS,))],
-        compiler_params=pltpu.CompilerParams(vmem_limit_bytes=48 << 20),
+        compiler_params=pltpu.CompilerParams(vmem_limit_bytes=30 << 20),
         cost_estimate=pl.CostEstimate(flops=5_000_000_000, bytes_accessed=6_000_000, transcendentals=8_000_000),
         name="block",
     )(*operands)
@@ -259,7 +259,7 @@
         out_shape=jax.ShapeDtypeStruct(x.shape, x.dtype),
         in_specs=[vmem, vmem],
         out_specs=vmem,
-        compiler_params=pltpu.CompilerParams(vmem_limit_bytes=32 << 20),
+        compiler_params=pltpu.CompilerParams(vmem_limit_bytes=16 << 20),
         cost_estimate=pl.CostEstimate(flops=1_100_000_000, bytes_accessed=2_100_000, transcendentals=0),
         name="permute",
     )(x, source.reshape(-1, 1))
@@ -296,32 +296,26 @@
         in_specs=[vmem],
         out_specs=(vmem, vmem),
         scratch_shapes=[pltpu.VMEM((rows, width), jnp.bfloat16)],
-        compiler_params=pltpu.CompilerParams(vmem_limit_bytes=32 << 20),
+        compiler_params=pltpu.CompilerParams(vmem_limit_bytes=16 << 20),
         cost_estimate=pl.CostEstimate(flops=1_100_000_000, bytes_accessed=2_200_000, transcendentals=0),
         name="regroup",
     )(x)
 
 
-def pick_kernel(source_ref, x_ref, out_ref, sems):
-    copies = [
-        pltpu.make_async_copy(x_ref.at[source_ref[q]], out_ref.at[q], sems.at[q]) for q in range(out_ref.shape[0])
-    ]
-    for copy in copies:
-        copy.start()
-    for copy in copies:
-        copy.wait()
+def pick_kernel(source_ref, x_ref, out_ref):
+    for q in range(out_ref.shape[0]):
+        out_ref[q] = x_ref[source_ref[q]]
 
 
 def pick_parts(x, source):
-    count = source.shape[0]
+    vmem = pl.BlockSpec(memory_space=pltpu.VMEM)
     return pl.pallas_call(
         pick_kernel,
-        out_shape=jax.ShapeDtypeStruct((count,) + x.shape[1:], x.dtype),
-        in_specs=[pl.BlockSpec(memory_space=pltpu.SMEM), pl.BlockSpec(memory_space=pl.ANY)],
-        out_specs=pl.BlockSpec(memory_space=pltpu.VMEM),
-        scratch_shapes=[pltpu.SemaphoreType.DMA((count,))],
-        compiler_params=pltpu.CompilerParams(vmem_limit_bytes=32 << 20),
-        cost_estimate=pl.CostEstimate(flops=0, bytes_accessed=2_100_000, transcendentals=0),
+        out_shape=jax.ShapeDtypeStruct((source.shape[0],) + x.shape[1:], x.dtype),
+        in_specs=[pl.BlockSpec(memory_space=pltpu.SMEM), vmem],
+        out_specs=vmem,
+        compiler_params=pltpu.CompilerParams(vmem_limit_bytes=16 << 20),
+        cost_estimate=pl.CostEstimate(flops=0, bytes_accessed=2_300_000, transcendentals=0),
         name="pick",
     )(source, x)
 
@@ -349,7 +343,7 @@
         out_shape=jax.ShapeDtypeStruct((groups, slots, rows // groups, width), x.dtype),
         in_specs=[smem, smem, vmem],
         out_specs=vmem,
-        compiler_params=pltpu.CompilerParams(vmem_limit_bytes=32 << 20),
+        compiler_params=pltpu.CompilerParams(vmem_limit_bytes=16 << 20),
         cost_estimate=pl.CostEstimate(flops=270_000_000, bytes_accessed=3_200_000, transcendentals=0),
         name="homeward",
     )(owner, live, x)

time: 321 us -> 318 us (level)
  no operation moved by 1% of the time
where the time goes in v4:
time: 318 us
  blocking collectives  106 us (33%)
  waiting for transfers between devices  95.6 us (30%)
  Pallas kernels  76.1 us (24%)
  starting transfers between devices  27.3 us (9%)
  local copies, waits for them, and re-layouts  8.94 us (3%)
    all_to_all x3, blocking collectives, exchange(): return lax.all_to_all(x, axis, split_axis=0, concat_axis=0, tiled=True)  106 us
    all_to_all x4, waiting for transfers between devices, exchange(): return lax.all_to_all(x, axis, split_axis=0, concat_axis=0, tiled=True)  95.6 us
    pallas_call x2, Pallas kernels, encoder_block(): pl.pallas_call(functools.partial(block_kernel, first), out_shape=jax.Shap...  69.7 us
    all_to_all x4, starting transfers between devices, exchange(): return lax.all_to_all(x, axis, split_axis=0, concat_axis=0, tiled=True)  27.3 us
  transfers between devices with their start and end apart: 4, of which 4 were waited for; matrix products, arithmetic and copies ran while one was open for 1% of the time, Pallas kernels for 0%

profile of v4, /device:TPU:1, one launch (start us, length us, event | category | flops | bytes accessed | tf_op | source)
XLA Modules:
  0.0 317.8 jit_solution(7553883112585673818)
XLA Ops:
  0.8 0.7 pad_add_fusion
  1.5 1.1 reshape.268
  2.7 0.1 copy.75
  2.8 0.9 fusion.1
  3.7 0.3 pad_maximum_fusion
  4.1 0.2 maximum_bitcast_fusion
  4.3 0.2 copy.61
  4.5 35.0 %all_to_all.35 = bf16[8,2,144,512]{3,2,1,0:T(8,128)(2,1)S(1)} all-to-all(bf16[8,2,144,512]{3,2,1,0:T(8,128)(2,1)S(1)} %copy.61), channel_id=1, replica_groups=mesh['grp'=8,'dev'=32] {'grp'}, dimensions={0} | all-to-all | bytes 4718592 | tf_op jit(solution)/shard_map/all_to_all | solution.py:353
  39.5 0.1 copy.70
  39.6 0.1 copy.63
  39.7 0.1 reshape.270.owner_ref
  39.8 0.1 iota_compare_fusion.1
  39.9 0.1 lt.52
  40.0 0.1 select_reduce_fusion.source_ref
  40.1 1.6 pick.1
  41.8 4.6 %all-to-all-start.1 = ((bf16[8,144,512]{2,1,0:T(8,128)(2,1)}), bf16[8,144,512]{2,1,0:T(8,128)(2,1)S(1)}, u32[]{:S(2)}, u32[]{:S(2)}) async-start(bf16[8,144,512]{2,1,0:T(8,128)(2,1)} %pick.1), calls=%async_computation.1 | async-start | bytes 2359296 | tf_op jit(solution)/shard_map/all_to_all | solution.py:353
  46.4 0.1 iota_add_fusion.1
  46.5 0.1 add.123
  46.6 0.1 pad.17.clone
  46.8 0.1 broadcast_in_dim.59
  46.9 0.1 broadcast_in_dim.54
  46.9 0.1 broadcast_in_dim.55
  47.1 15.9 %all-to-all-done.1.refs_0_ = bf16[8,144,512]{2,1,0:T(8,128)(2,1)S(1)} async-done(((bf16[8,144,512]{2,1,0:T(8,128)(2,1)}), bf16[8,144,512]{2,1,0:T(8,128)(2,1)S(1)}, u32[]{:S(2)}, u32[]{:S(2)}) %all-to-all-start.1) | async-done | bytes 1179680 | tf_op jit(solution)/shard_map/all_to_all | solution.py:353
  63.0 1.4 copy-done
  64.4 34.8 %block.2 = bf16[32,136,128]{2,1,0:T(8,128)(2,1)S(1)} custom-call(bf16[8,144,512]{2,1,0:T(8,128)(2,1)S(1)} %all-to-all-done.1.refs_0_, bf16[8,128]{1,0:T(8,128)(2,1)S(1)} %select_convert_fusion.refs_1_, f32[27,4,128]{2,1,0:T(4,128)S(1)} %reshape.273.refs_2_, bf16[512,512]{1,0:T(8,128)(2,1)S(1)} %copy-done.2, f32[1,512]{1,0:T(1,128)S(1)} %bitcast.34, ...), custom_call_target="tpu_custom_call" | custom-call | flops 5000000000 | bytes 6000000 | tf_op jit(solution)/shard_map/block/pallas_call | solution.py:206
  99.2 40.7 %all_to_all.36.x_ref = bf16[32,136,128]{2,1,0:T(8,128)(2,1)S(1)} all-to-all(bf16[32,136,128]{2,1,0:T(8,128)(2,1)S(1)} %block.2), channel_id=1, replica_groups=mesh['grp'=8,'dev'=32] {'dev'}, dimensions={0} | all-to-all | bytes 2228224 | tf_op jit(solution)/shard_map/all_to_all | solution.py:353
  139.9 2.3 regroup.1
  142.2 5.0 %all-to-all-start.3 = ((bf16[32,32,512]{2,1,0:T(8,128)(2,1)}), bf16[32,32,512]{2,1,0:T(8,128)(2,1)S(1)}, u32[]{:S(2)}, u32[]{:S(2)}) async-start(bf16[32,32,512]{2,1,0:T(8,128)(2,1)} %bitcast.8), calls=%async_computation.3 | async-start | bytes 2097152 | tf_op jit(solution)/shard_map/all_to_all | solution.py:353
  147.2 0.1 fusion.4
  147.5 25.1 %all-to-all-done.3 = bf16[32,32,512]{2,1,0:T(8,128)(2,1)S(1)} async-done(((bf16[32,32,512]{2,1,0:T(8,128)(2,1)}), bf16[32,32,512]{2,1,0:T(8,128)(2,1)S(1)}, u32[]{:S(2)}, u32[]{:S(2)}) %all-to-all-start.3) | async-done | bytes 1048608 | tf_op jit(solution)/shard_map/all_to_all | solution.py:353
  172.6 1.4 copy-done.1
  174.0 34.9 %block.3 = bf16[1024,512]{1,0:T(8,128)(2,1)} custom-call(s32[8,32,128]{2,1,0:T(8,128)S(1)} %pad.14.refs_0_, bf16[1024,512]{1,0:T(8,128)(2,1)S(1)} %bitcast.33, f32[27,4,128]{2,1,0:T(4,128)S(1)} %reshape.277.refs_2_, bf16[512,512]{1,0:T(8,128)(2,1)S(1)} %copy-done.4, f32[1,512]{1,0:T(1,128)S(1)} %bitcast.35, bf16[512,1536]{1,0:T(8,128)(2,1)S(1)} %copy-done.1, ...), custom_call_target="tpu_custom_call" | custom-call | flops 5000000000 | bytes 6000000 | tf_op jit(solution)/shard_map/block/pallas_call | solution.py:206
  208.9 6.9 %all-to-all-start.4 = ((bf16[32,32,512]{2,1,0:T(8,128)(2,1)}), bf16[32,32,512]{2,1,0:T(8,128)(2,1)S(1)}, u32[]{:S(2)}, u32[]{:S(2)}) async-start(bf16[32,32,512]{2,1,0:T(8,128)(2,1)} %bitcast.11), calls=%async_computation.4 | async-start | bytes 2097152 | tf_op jit(solution)/shard_map/all_to_all | solution.py:353
  215.8 0.2 reshape_squeeze.3
  216.0 0.2 copy.65
  216.2 0.1 copy.66
  216.3 0.1 mul.38
  216.5 0.1 iota_add_fusion
  216.6 0.1 add.129.source_ref
  216.8 23.6 %all-to-all-done.4 = bf16[32,32,512]{2,1,0:T(8,128)(2,1)S(1)} async-done(((bf16[32,32,512]{2,1,0:T(8,128)(2,1)}), bf16[32,32,512]{2,1,0:T(8,128)(2,1)S(1)}, u32[]{:S(2)}, u32[]{:S(2)}) %all-to-all-start.4) | async-done | bytes 1048608 | tf_op jit(solution)/shard_map/all_to_all | solution.py:353
  240.3 1.3 permute.1
  241.6 1.1 reshape.281
  242.7 10.8 %all-to-all-start.5 = ((bf16[256,4,512]{2,1,0:T(4,128)(2,1)}), bf16[256,4,512]{2,1,0:T(4,128)(2,1)S(1)}, u32[]{:S(2)}, u32[]{:S(2)}) async-start(bf16[256,4,512]{2,1,0:T(4,128)(2,1)} %reshape.281), calls=%async_computation.5 | async-start | bytes 2097152 | tf_op jit(solution)/shard_map/all_to_all | solution.py:353
  253.5 31.2 %all-to-all-done.5 = bf16[256,4,512]{2,1,0:T(4,128)(2,1)S(1)} async-done(((bf16[256,4,512]{2,1,0:T(4,128)(2,1)}), bf16[256,4,512]{2,1,0:T(4,128)(2,1)S(1)}, u32[]{:S(2)}, u32[]{:S(2)}) %all-to-all-start.5) | async-done | bytes 1048608 | tf_op jit(solution)/shard_map/all_to_all | solution.py:353
  284.7 0.3 reshape.282.x_ref
  285.0 1.2 homeward.1
  286.2 30.0 %all_to_all.37 = bf16[8,2,128,512]{3,2,1,0:T(8,128)(2,1)S(1)} all-to-all(bf16[8,2,128,512]{3,2,1,0:T(8,128)(2,1)S(1)} %homeward.1), channel_id=1, replica_groups=mesh['grp'=8,'dev'=32] {'grp'}, dimensions={0} | all-to-all | bytes 4194304 | tf_op jit(solution)/shard_map/all_to_all | solution.py:353
  316.2 1.5 copy.68
  (48 shorter events, 0.4 us)
Async XLA Ops:
  0.0 4.1 %copy-start.8 = (bf16[2048,512]{1,0:T(8,128)(2,1)S(1)}, bf16[2048,512]{1,0:T(8,128)(2,1)}, u32[]{:S(2)}) copy-start(bf16[2048,512]{1,0:T(8,128)(2,1)} %param.16) | copy-start | bytes 6291460
  40.1 6.3 %copy-start.12 = (s32[16]{0:T(128)S(1)}, s32[16]{0:T(128)}, u32[]{:S(2)}) copy-start(s32[16]{0:T(128)} %param.20) | copy-start | bytes 196
  40.1 6.9 %copy-start.10 = (f32[27,512]{1,0:T(8,128)S(1)}, f32[27,512]{1,0:T(8,128)}, u32[]{:S(2)}) copy-start(f32[27,512]{1,0:T(8,128)} %param.22) | copy-start | bytes 165892
  40.1 22.8 %copy-start.2 = (bf16[512,512]{1,0:T(8,128)(2,1)S(1)}, bf16[512,512]{1,0:T(8,128)(2,1)}, u32[]{:S(2)}) copy-start(bf16[512,512]{1,0:T(8,128)(2,1)} %refs_3_.2) | copy-start | bytes 1572868
  40.1 22.8 %copy-start.6 = (f32[512]{0:T(512)S(1)}, f32[512]{0:T(512)}, u32[]{:S(2)}) copy-start(f32[512]{0:T(512)} %param.24) | copy-start | bytes 6148
  41.8 21.2 %copy-start.3 = (bf16[512,512]{1,0:T(8,128)(2,1)S(1)}, bf16[512,512]{1,0:T(8,128)(2,1)}, u32[]{:S(2)}) copy-start(bf16[512,512]{1,0:T(8,128)(2,1)} %refs_6_.2) | copy-start | bytes 1572868
  41.8 21.2 %all-to-all-start.1 = ((bf16[8,144,512]{2,1,0:T(8,128)(2,1)}), bf16[8,144,512]{2,1,0:T(8,128)(2,1)S(1)}, u32[]{:S(2)}, u32[]{:S(2)}) async-start(bf16[8,144,512]{2,1,0:T(8,128)(2,1)} %pick.1), calls=%async_computation.1 | async-start | bytes 2359296 | tf_op jit(solution)/shard_map/all_to_all | solution.py:353
  62.9 1.4 copy-start
  139.9 7.3 %copy-start.9 = (s32[27,1024]{1,0:T(8,128)S(1)}, s32[27,1024]{1,0:T(8,128)}, u32[]{:S(2)}) copy-start(s32[27,1024]{1,0:T(8,128)} %param.21) | copy-start | bytes 331780
  142.2 5.3 %copy-start.11 = (f32[27,512]{1,0:T(8,128)S(1)}, f32[27,512]{1,0:T(8,128)}, u32[]{:S(2)}) copy-start(f32[27,512]{1,0:T(8,128)} %param.27) | copy-start | bytes 165892
  142.2 30.4 %copy-start.4 = (bf16[512,512]{1,0:T(8,128)(2,1)S(1)}, bf16[512,512]{1,0:T(8,128)(2,1)}, u32[]{:S(2)}) copy-start(bf16[512,512]{1,0:T(8,128)(2,1)} %refs_3_.3) | copy-start | bytes 1572868
  142.2 30.4 %copy-start.5 = (bf16[512,512]{1,0:T(8,128)(2,1)S(1)}, bf16[512,512]{1,0:T(8,128)(2,1)}, u32[]{:S(2)}) copy-start(bf16[512,512]{1,0:T(8,128)(2,1)} %refs_6_.3) | copy-start | bytes 1572868
  142.2 30.4 %copy-start.7 = (f32[512]{0:T(512)S(1)}, f32[512]{0:T(512)}, u32[]{:S(2)}) copy-start(f32[512]{0:T(512)} %param.29) | copy-start | bytes 6148
  142.2 30.4 %all-to-all-start.3 = ((bf16[32,32,512]{2,1,0:T(8,128)(2,1)}), bf16[32,32,512]{2,1,0:T(8,128)(2,1)S(1)}, u32[]{:S(2)}, u32[]{:S(2)}) async-start(bf16[32,32,512]{2,1,0:T(8,128)(2,1)} %bitcast.8), calls=%async_computation.3 | async-start | bytes 2097152 | tf_op jit(solution)/shard_map/all_to_all | solution.py:353
  172.6 1.4 copy-start.1
  208.9 31.5 %all-to-all-start.4 = ((bf16[32,32,512]{2,1,0:T(8,128)(2,1)}), bf16[32,32,512]{2,1,0:T(8,128)(2,1)S(1)}, u32[]{:S(2)}, u32[]{:S(2)}) async-start(bf16[32,32,512]{2,1,0:T(8,128)(2,1)} %bitcast.11), calls=%async_computation.4 | async-start | bytes 2097152 | tf_op jit(solution)/shard_map/all_to_all | solution.py:353
  242.7 42.0 %all-to-all-start.5 = ((bf16[256,4,512]{2,1,0:T(4,128)(2,1)}), bf16[256,4,512]{2,1,0:T(4,128)(2,1)S(1)}, u32[]{:S(2)}, u32[]{:S(2)}) async-start(bf16[256,4,512]{2,1,0:T(4,128)(2,1)} %reshape.281), calls=%async_computation.5 | async-start | bytes 2097152 | tf_op jit(solution)/shard_map/all_to_all | solution.py:353

commit v5 on v4

--- a/solution.py
+++ b/solution.py
@@ -22,12 +22,12 @@
 def block_kernel(first, *refs):
     if first:
         (
-            x_ref, note_ref, depth_ref, mixing_ref, gain_ref, w_qkv_ref, w_out_ref, out_ref,
+            x_ref, note_ref, depth_ref, mixing_ref, gain_ref, w_q_ref, w_k_ref, w_v_ref, w_out_ref, out_ref,
             plain, summed, updated, project, mixed, scores_even, scores_odd, powers_even, powers_odd, lists_ref, *stage
         ) = refs
     else:
         (
-            lists_ref, x_ref, depth_ref, mixing_ref, gain_ref, w_qkv_ref, w_out_ref, out_ref,
+            lists_ref, x_ref, depth_ref, mixing_ref, gain_ref, w_q_ref, w_k_ref, w_v_ref, w_out_ref, out_ref,
             plain, summed, updated, project, mixed, scores_even, scores_odd, powers_even, powers_odd, *stage
         ) = refs
     buffers, sems = stage[:BUFFERS], stage[BUFFERS]
@@ -119,11 +119,12 @@
         spread = jnp.mean(off * off, axis=-1, keepdims=True)
         normed = (off * lax.rsqrt(spread + epsilon) * gain_ref[...]).astype(jnp.bfloat16)
         project[pl.ds(row0, TILE), :width] = (
-            jnp.dot(normed, w_qkv_ref[:, :width], preferred_element_type=jnp.float32) * SCALE
+            jnp.dot(normed, w_q_ref[...], preferred_element_type=jnp.float32) * SCALE
         ).astype(jnp.bfloat16)
-        project[pl.ds(row0, TILE), width:] = jnp.dot(
-            normed, w_qkv_ref[:, width:], preferred_element_type=jnp.float32
-        ).astype(jnp.bfloat16)
+        for side, w_ref in ((1, w_k_ref), (2, w_v_ref)):
+            project[pl.ds(row0, TILE), side * width : (side + 1) * width] = jnp.dot(
+                normed, w_ref[...], preferred_element_type=jnp.float32
+            ).astype(jnp.bfloat16)
         return carry
 
     lax.fori_loop(0, tiles, head, 0)
@@ -200,7 +201,7 @@
     fanout, width = depth.shape
     vmem = pl.BlockSpec(memory_space=pltpu.VMEM)
     table = (rows // CHUNK, SIDE, LANES)
-    operands = (depth.reshape(fanout, -1, LANES), mixing, gain.reshape(1, width), w_qkv, w_out)
+    operands = (depth.reshape(fanout, -1, LANES), mixing, gain.reshape(1, width), *jnp.split(w_qkv, 3, axis=1), w_out)
     operands = ((features, beside) if first else (beside, features)) + operands
     shape = (rows // SIDE, SIDE * width // LANES + NOTE_ROWS, LANES) if first else (rows, width)
     return pl.pallas_call(

time: 318 us -> 319 us (level)
  blocking collectives: 106 us -> 69.8 us
  waiting for transfers between devices: 95.6 us -> 122 us
  starting transfers between devices: 27.3 us -> 33.9 us
  local copies, waits for them, and re-layouts: 8.94 us -> 12.7 us
    all_to_all x3 -> x2, blocking collectives: 106 us -> 69.8 us  [exchange(): return lax.all_to_all(x, axis, split_axis=0, concat_axis=0, tiled=True)]
    all_to_all x4 -> x5, waiting for transfers between devices: 95.6 us -> 122 us  [exchange(): return lax.all_to_all(x, axis, split_axis=0, concat_axis=0, tiled=True)]
    all_to_all x4 -> x5, starting transfers between devices: 27.3 us -> 33.9 us  [exchange(): return lax.all_to_all(x, axis, split_axis=0, concat_axis=0, tiled=True)]
  transfers between devices with their start and end apart: 4 -> 5, of which waited for: 4 -> 5; matrix products, arithmetic and copies ran while one was open for 1% -> 1% of each run, Pallas kernels for 0% -> 0%
where the time goes in v5:
time: 319 us; the launch traced here: 318 us
  waiting for transfers between devices  122 us (38%)
  Pallas kernels  76.2 us (24%)
  blocking collectives  69.8 us (22%)
  starting transfers between devices  33.9 us (11%)
  local copies, waits for them, and re-layouts  12.7 us (4%)
    all_to_all x5, waiting for transfers between devices, exchange(): return lax.all_to_all(x, axis, split_axis=0, concat_axis=0, tiled=True)  122 us
    all_to_all x2, blocking collectives, exchange(): return lax.all_to_all(x, axis, split_axis=0, concat_axis=0, tiled=True)  69.8 us
    pallas_call x2, Pallas kernels, encoder_block(): pl.pallas_call(functools.partial(block_kernel, first), out_shape=jax.Shap...  69.7 us
    all_to_all x5, starting transfers between devices, exchange(): return lax.all_to_all(x, axis, split_axis=0, concat_axis=0, tiled=True)  33.9 us
  transfers between devices with their start and end apart: 5, of which 5 were waited for; matrix products, arithmetic and copies ran while one was open for 1% of the time, Pallas kernels for 0%

profile of v5, /device:TPU:1, one launch (start us, length us, event | category | flops | bytes accessed | tf_op | source)
XLA Modules:
  0.0 318.3 jit_solution(14061755370015417185)
XLA Ops:
  0.8 0.7 pad_add_fusion
  1.5 1.1 reshape.268
  2.7 0.1 copy.75
  2.8 0.9 fusion.1
  3.7 0.3 pad_maximum_fusion
  4.1 0.2 maximum_bitcast_fusion
  4.3 1.6 copy.61
  6.0 6.9 %all-to-all-start = ((bf16[8,2,144,512]{3,2,1,0:T(8,128)(2,1)}), bf16[8,2,144,512]{3,2,1,0:T(8,128)(2,1)S(1)}, u32[]{:S(2)}, u32[]{:S(2)}) async-start(bf16[8,2,144,512]{3,2,1,0:T(8,128)(2,1)} %copy.61), calls=%async_computation | async-start | bytes 4718592 | tf_op jit(solution)/shard_map/all_to_all | solution.py:354
  12.9 0.1 add.123
  13.1 28.9 %all-to-all-done = bf16[8,2,144,512]{3,2,1,0:T(8,128)(2,1)S(1)} async-done(((bf16[8,2,144,512]{3,2,1,0:T(8,128)(2,1)}), bf16[8,2,144,512]{3,2,1,0:T(8,128)(2,1)S(1)}, u32[]{:S(2)}, u32[]{:S(2)}) %all-to-all-start) | async-done | bytes 2359328 | tf_op jit(solution)/shard_map/all_to_all | solution.py:354
  42.0 0.1 copy.70
  42.2 0.1 copy.63
  42.2 0.1 reshape.270.owner_ref
  42.4 0.1 lt.52
  42.5 0.1 select_reduce_fusion.source_ref
  42.6 1.6 pick.1
  44.2 4.3 %all-to-all-start.1 = ((bf16[8,144,512]{2,1,0:T(8,128)(2,1)}), bf16[8,144,512]{2,1,0:T(8,128)(2,1)S(1)}, u32[]{:S(2)}, u32[]{:S(2)}) async-start(bf16[8,144,512]{2,1,0:T(8,128)(2,1)} %pick.1), calls=%async_computation.1 | async-start | bytes 2359296 | tf_op jit(solution)/shard_map/all_to_all | solution.py:354
  48.7 0.1 broadcast_in_dim.59
  48.8 0.1 broadcast_in_dim.54
  48.8 0.1 broadcast_in_dim.55
  49.0 1.5 fusion.11
  50.5 14.7 %all-to-all-done.1.refs_0_ = bf16[8,144,512]{2,1,0:T(8,128)(2,1)S(1)} async-done(((bf16[8,144,512]{2,1,0:T(8,128)(2,1)}), bf16[8,144,512]{2,1,0:T(8,128)(2,1)S(1)}, u32[]{:S(2)}, u32[]{:S(2)}) %all-to-all-start.1) | async-done | bytes 1179680 | tf_op jit(solution)/shard_map/all_to_all | solution.py:354
  65.1 1.0 copy-done.1
  66.2 34.9 %block.2 = bf16[32,136,128]{2,1,0:T(8,128)(2,1)S(1)} custom-call(bf16[8,144,512]{2,1,0:T(8,128)(2,1)S(1)} %all-to-all-done.1.refs_0_, bf16[8,128]{1,0:T(8,128)(2,1)S(1)} %select_convert_fusion.refs_1_, f32[27,4,128]{2,1,0:T(4,128)S(1)} %reshape.273.refs_2_, bf16[512,512]{1,0:T(8,128)(2,1)S(1)} %copy-done, f32[1,512]{1,0:T(1,128)S(1)} %bitcast.34, ...), custom_call_target="tpu_custom_call" | custom-call | flops 5000000000 | bytes 6000000 | tf_op jit(solution)/shard_map/block/pallas_call | solution.py:207
  101.1 39.8 %all_to_all.35.x_ref = bf16[32,136,128]{2,1,0:T(8,128)(2,1)S(1)} all-to-all(bf16[32,136,128]{2,1,0:T(8,128)(2,1)S(1)} %block.2), channel_id=1, replica_groups=mesh['grp'=8,'dev'=32] {'dev'}, dimensions={0} | all-to-all | bytes 2228224 | tf_op jit(solution)/shard_map/all_to_all | solution.py:354
  140.9 2.3 regroup.1
  143.2 5.0 %all-to-all-start.3 = ((bf16[32,32,512]{2,1,0:T(8,128)(2,1)}), bf16[32,32,512]{2,1,0:T(8,128)(2,1)S(1)}, u32[]{:S(2)}, u32[]{:S(2)}) async-start(bf16[32,32,512]{2,1,0:T(8,128)(2,1)} %bitcast.8), calls=%async_computation.3 | async-start | bytes 2097152 | tf_op jit(solution)/shard_map/all_to_all | solution.py:354
  148.2 0.1 fusion.4
  148.5 1.5 fusion.10
  150.0 23.6 %all-to-all-done.3 = bf16[32,32,512]{2,1,0:T(8,128)(2,1)S(1)} async-done(((bf16[32,32,512]{2,1,0:T(8,128)(2,1)}), bf16[32,32,512]{2,1,0:T(8,128)(2,1)S(1)}, u32[]{:S(2)}, u32[]{:S(2)}) %all-to-all-start.3) | async-done | bytes 1048608 | tf_op jit(solution)/shard_map/all_to_all | solution.py:354
  173.5 1.0 copy-done.3
  174.6 34.8 %block.3 = bf16[1024,512]{1,0:T(8,128)(2,1)} custom-call(s32[8,32,128]{2,1,0:T(8,128)S(1)} %pad.14.refs_0_, bf16[1024,512]{1,0:T(8,128)(2,1)S(1)} %bitcast.33, f32[27,4,128]{2,1,0:T(4,128)S(1)} %reshape.277.refs_2_, bf16[512,512]{1,0:T(8,128)(2,1)S(1)} %copy-done.2, f32[1,512]{1,0:T(1,128)S(1)} %bitcast.35, bf16[512,512]{1,0:T(8,128)(2,1)S(1)} %get-tuple-element.10.refs_5_, ...), custom_call_target="tpu_custom_call" | custom-call | flops 5000000000 | bytes 6000000 | tf_op jit(solution)/shard_map/block/pallas_call | solution.py:207
  209.4 6.9 %all-to-all-start.4 = ((bf16[32,32,512]{2,1,0:T(8,128)(2,1)}), bf16[32,32,512]{2,1,0:T(8,128)(2,1)S(1)}, u32[]{:S(2)}, u32[]{:S(2)}) async-start(bf16[32,32,512]{2,1,0:T(8,128)(2,1)} %bitcast.11), calls=%async_computation.4 | async-start | bytes 2097152 | tf_op jit(solution)/shard_map/all_to_all | solution.py:354
  216.3 0.2 reshape_squeeze.3
  216.5 0.2 copy.65
  216.7 0.1 copy.66
  216.9 0.1 mul.38
  217.0 0.1 iota_add_fusion
  217.1 0.1 add.129.source_ref
  217.3 23.5 %all-to-all-done.4 = bf16[32,32,512]{2,1,0:T(8,128)(2,1)S(1)} async-done(((bf16[32,32,512]{2,1,0:T(8,128)(2,1)}), bf16[32,32,512]{2,1,0:T(8,128)(2,1)S(1)}, u32[]{:S(2)}, u32[]{:S(2)}) %all-to-all-start.4) | async-done | bytes 1048608 | tf_op jit(solution)/shard_map/all_to_all | solution.py:354
  240.8 1.3 permute.1
  242.1 1.1 reshape.281
  243.2 10.8 %all-to-all-start.5 = ((bf16[256,4,512]{2,1,0:T(4,128)(2,1)}), bf16[256,4,512]{2,1,0:T(4,128)(2,1)S(1)}, u32[]{:S(2)}, u32[]{:S(2)}) async-start(bf16[256,4,512]{2,1,0:T(4,128)(2,1)} %reshape.281), calls=%async_computation.5 | async-start | bytes 2097152 | tf_op jit(solution)/shard_map/all_to_all | solution.py:354
  254.1 31.2 %all-to-all-done.5 = bf16[256,4,512]{2,1,0:T(4,128)(2,1)S(1)} async-done(((bf16[256,4,512]{2,1,0:T(4,128)(2,1)}), bf16[256,4,512]{2,1,0:T(4,128)(2,1)S(1)}, u32[]{:S(2)}, u32[]{:S(2)}) %all-to-all-start.5) | async-done | bytes 1048608 | tf_op jit(solution)/shard_map/all_to_all | solution.py:354
  285.2 0.3 reshape.282.x_ref
  285.5 1.2 homeward.1
  286.8 30.0 %all_to_all.36 = bf16[8,2,128,512]{3,2,1,0:T(8,128)(2,1)S(1)} all-to-all(bf16[8,2,128,512]{3,2,1,0:T(8,128)(2,1)S(1)} %homeward.1), channel_id=1, replica_groups=mesh['grp'=8,'dev'=32] {'grp'}, dimensions={0} | all-to-all | bytes 4194304 | tf_op jit(solution)/shard_map/all_to_all | solution.py:354
  316.8 1.5 copy.68
  (47 shorter events, 0.6 us)
Async XLA Ops:
  0.0 4.1 %copy-start.6 = (bf16[2048,512]{1,0:T(8,128)(2,1)S(1)}, bf16[2048,512]{1,0:T(8,128)(2,1)}, u32[]{:S(2)}) copy-start(bf16[2048,512]{1,0:T(8,128)(2,1)} %param.16) | copy-start | bytes 6291460
  6.0 6.9 %copy-start.10 = (s32[16]{0:T(128)S(1)}, s32[16]{0:T(128)}, u32[]{:S(2)}) copy-start(s32[16]{0:T(128)} %param.20) | copy-start | bytes 196
  6.0 36.1 %all-to-all-start = ((bf16[8,2,144,512]{3,2,1,0:T(8,128)(2,1)}), bf16[8,2,144,512]{3,2,1,0:T(8,128)(2,1)S(1)}, u32[]{:S(2)}, u32[]{:S(2)}) async-start(bf16[8,2,144,512]{3,2,1,0:T(8,128)(2,1)} %copy.61), calls=%async_computation | async-start | bytes 4718592 | tf_op jit(solution)/shard_map/all_to_all | solution.py:354
  42.6 6.3 %copy-start.8 = (f32[27,512]{1,0:T(8,128)S(1)}, f32[27,512]{1,0:T(8,128)}, u32[]{:S(2)}) copy-start(f32[27,512]{1,0:T(8,128)} %param.22) | copy-start | bytes 165892
  44.2 20.9 %all-to-all-start.1 = ((bf16[8,144,512]{2,1,0:T(8,128)(2,1)}), bf16[8,144,512]{2,1,0:T(8,128)(2,1)S(1)}, u32[]{:S(2)}, u32[]{:S(2)}) async-start(bf16[8,144,512]{2,1,0:T(8,128)(2,1)} %pick.1), calls=%async_computation.1 | async-start | bytes 2359296 | tf_op jit(solution)/shard_map/all_to_all | solution.py:354
  48.6 16.5 %copy-start = (bf16[512,512]{1,0:T(8,128)(2,1)S(1)}, bf16[512,512]{1,0:T(8,128)(2,1)}, u32[]{:S(2)}) copy-start(bf16[512,512]{1,0:T(8,128)(2,1)} %refs_3_.2) | copy-start | bytes 1572868
  48.6 16.5 %copy-start.4 = (f32[512]{0:T(512)S(1)}, f32[512]{0:T(512)}, u32[]{:S(2)}) copy-start(f32[512]{0:T(512)} %param.24) | copy-start | bytes 6148
  65.1 1.0 copy-start.1
  140.9 7.3 %copy-start.7 = (s32[27,1024]{1,0:T(8,128)S(1)}, s32[27,1024]{1,0:T(8,128)}, u32[]{:S(2)}) copy-start(s32[27,1024]{1,0:T(8,128)} %param.21) | copy-start | bytes 331780
  143.2 5.3 %copy-start.9 = (f32[27,512]{1,0:T(8,128)S(1)}, f32[27,512]{1,0:T(8,128)}, u32[]{:S(2)}) copy-start(f32[27,512]{1,0:T(8,128)} %param.27) | copy-start | bytes 165892
  143.2 30.3 %all-to-all-start.3 = ((bf16[32,32,512]{2,1,0:T(8,128)(2,1)}), bf16[32,32,512]{2,1,0:T(8,128)(2,1)S(1)}, u32[]{:S(2)}, u32[]{:S(2)}) async-start(bf16[32,32,512]{2,1,0:T(8,128)(2,1)} %bitcast.8), calls=%async_computation.3 | async-start | bytes 2097152 | tf_op jit(solution)/shard_map/all_to_all | solution.py:354
  148.3 25.2 %copy-start.2 = (bf16[512,512]{1,0:T(8,128)(2,1)S(1)}, bf16[512,512]{1,0:T(8,128)(2,1)}, u32[]{:S(2)}) copy-start(bf16[512,512]{1,0:T(8,128)(2,1)} %refs_3_.3) | copy-start | bytes 1572868
  148.3 25.2 %copy-start.5 = (f32[512]{0:T(512)S(1)}, f32[512]{0:T(512)}, u32[]{:S(2)}) copy-start(f32[512]{0:T(512)} %param.29) | copy-start | bytes 6148
  173.5 1.0 copy-start.3
  209.4 31.4 %all-to-all-start.4 = ((bf16[32,32,512]{2,1,0:T(8,128)(2,1)}), bf16[32,32,512]{2,1,0:T(8,128)(2,1)S(1)}, u32[]{:S(2)}, u32[]{:S(2)}) async-start(bf16[32,32,512]{2,1,0:T(8,128)(2,1)} %bitcast.11), calls=%async_computation.4 | async-start | bytes 2097152 | tf_op jit(solution)/shard_map/all_to_all | solution.py:354
  243.2 42.0 %all-to-all-start.5 = ((bf16[256,4,512]{2,1,0:T(4,128)(2,1)}), bf16[256,4,512]{2,1,0:T(4,128)(2,1)S(1)}, u32[]{:S(2)}, u32[]{:S(2)}) async-start(bf16[256,4,512]{2,1,0:T(4,128)(2,1)} %reshape.281), calls=%async_computation.5 | async-start | bytes 2097152 | tf_op jit(solution)/shard_map/all_to_all | solution.py:354
